TPU v7x, 512 devices: a whole 4x4x16 slice. The times are simulated.
512 devices in a mesh: ev: 64 (over y, z_lo, core), tile: 8 (over x, z_hi).
Axes of the slice: x: 4, y: 4, z: 16 (z_hi: 2, z_lo: 8; z = z_hi * 8 + z_lo), core: 2. Of those that a mesh axis runs over, the one named last changes fastest.
Arguments:
- phase_times: float32 [8, 128, 256], P('tile', 'ev'), may hold values from -512 to 512
- kernel_ids: int32 [8, 128, 256], P('tile', 'ev'), may hold values from 0 to 63
- block_ids: int32 [8, 128, 256], P('tile', 'ev'), may hold values from 0 to 1023
- dest_tiles: int32 [8, 128, 256, 1], P('tile', 'ev'), may hold values from 0 to 7; in each aligned block of 512 rows (0 to 511, 512 to 1023, ..., all dimensions but the last counted through in order) at most 128 rows name the same one
- station_counts: int32 [8, 128], P('tile', 'ev'), may hold values from 1 to 256, 24576 in all within a row
- weight_table: int32 [64, 128], replicated, may hold values from 1 to 256
- source_row: float32 [128], P('ev'), may hold values from -1024 to -128
- source_col: float32 [128], P('ev'), may hold values from 0 to 2048
- valid_cells: float32 [128, 512, 2048], P('ev', None, 'tile'), may hold values from 0 to 1
Outputs:
- slowness: float32 [512, 2048], P('ev', 'tile')
Inputs may be any that keep to these rules, and one draw needn't show every extreme that they name: `dest_tiles`: among the 512 slots of one list part held by one device (its events, its index of tile, in order), no map tile is named by more than 128 slots, and in every draw some tile is named by exactly 128 of one device's slots. `station_counts`: in each list the counts over all events sum to 24576, and some event has all 256 slots live.
All inputs are finite; a program needn't handle non-finite values. No bound on the sum of `station_counts` on one device may be relied on, other than what follows from the above.
Results may differ from a plain program's by a relative error of at most 0.0003.
Values sent between devices are 32-bit elements; how exact they have to be, the bound alone decides.
No kernel may reach another device: no remote copies, remote signals or barrier semaphores. Data moves between devices by JAX's collectives and lax.ppermute only.
A program may use at most 64 MiB of HBM per device.

v0:
```python
import jax
import jax.numpy as jnp
from jax import lax
from jax.sharding import PartitionSpec as P

SWEEPS = 4


SMOOTH = 0.024


def extended(x, sides, width):
    for axis, dim in sides:
        size, length = (lax.axis_size(axis), x.shape[dim])
        up = [(i, (i + 1) % size) for i in range(size - 1)]
        down = [(j, i) for i, j in up]
        last = lax.slice_in_dim(x, length - width, length, axis=dim)
        initial = lax.slice_in_dim(x, 0, width, axis=dim)
        before = lax.ppermute(last, axis, up)
        after = lax.ppermute(initial, axis, down)
        x = jnp.concatenate([before, x, after], axis=dim)
    return x


def laplace(values):
    padded = jnp.pad(values, ((0, 0), (1, 1), (1, 1)))
    beside_all = (
        padded[:, :-2, 1:-1] + padded[:, 2:, 1:-1] + padded[:, 1:-1, :-2] + padded[:, 1:-1, 2:]
    )
    return beside_all - 4.0 * values


def sweep_once(change, numerator, weight_sum, inside):
    curvature = laplace(change) * inside
    bending = laplace(curvature)
    return (change - SMOOTH * (bending + weight_sum * change - numerator)) * inside


def speed_field(margin, row_pos, col_pos, src_rows, src_cols):
    rows_padded = jnp.pad(margin, ((0, 0), (1, 1), (0, 0)))
    grad_row = 0.5 * (rows_padded[:, 2:, 1:-1] - rows_padded[:, :-2, 1:-1])
    grad_col = 0.5 * (margin[:, :, 2:] - margin[:, :, :-2])
    off_row = row_pos[None, :, None] - src_rows[:, None, None]
    off_col = col_pos[None, None, :] - src_cols[:, None, None]
    distance = jnp.sqrt(off_row * off_row + off_col * off_col)
    along_row = off_row / distance + grad_row
    along_col = off_col / distance + grad_col
    return jnp.sqrt(along_row * along_row + along_col * along_col)


def on_device(
    phase_times,
    kernel_ids,
    block_ids,
    dest_tiles,
    station_counts,
    weight_table,
    source_row,
    source_col,
    valid_cells,
):
    tile_count = lax.axis_size("tile")
    tile_index = lax.axis_index("tile")
    local_events, rows_all, local_cols = valid_cells.shape
    slot_count = phase_times.shape[2]
    blocks = rows_all * local_cols // 128
    live_slot = jnp.arange(slot_count, dtype=jnp.int32)[None, :] < station_counts[0][:, None]
    kernel_send = jnp.where(live_slot, kernel_ids[0], -1).reshape(-1)
    target = dest_tiles[0, :, :, 0].reshape(-1)
    cell_block = (
        jnp.arange(local_events, dtype=jnp.int32)[:, None] * blocks + block_ids[0]
    ).reshape(-1)
    times_flat = phase_times[0].reshape(-1)
    capacity = 2 * local_events * slot_count // tile_count
    chosen = (target[:, None] == jnp.arange(tile_count, dtype=jnp.int32)[None, :]).astype(jnp.int32)
    before = jnp.cumsum(chosen, axis=0) - chosen
    arrival_rank = jnp.sum(before * chosen, axis=1)
    position = target * capacity + arrival_rank
    payload = jnp.stack(
        [times_flat, kernel_send.astype(jnp.float32), cell_block.astype(jnp.float32)]
    )
    outgoing = jnp.zeros((3, tile_count * capacity), jnp.float32).at[1].set(-1.0)
    outgoing = outgoing.at[:, position].set(payload).reshape(3, tile_count, capacity)
    incoming = lax.all_to_all(outgoing, "tile", split_axis=1, concat_axis=1, tiled=True).reshape(
        3, -1
    )
    arrived_time = incoming[0]
    arrived_kernel = incoming[1].astype(jnp.int32)
    arrived_place = incoming[2].astype(jnp.int32)
    kernel_pick = (
        arrived_kernel[:, None] == jnp.arange(weight_table.shape[0], dtype=jnp.int32)[None, :]
    ).astype(jnp.bfloat16)
    weights = jnp.dot(
        kernel_pick, weight_table.astype(jnp.bfloat16), preferred_element_type=jnp.float32
    ) * (1.0 / 256.0)
    numerator = (
        jnp.zeros((local_events * blocks, 128), jnp.float32)
        .at[arrived_place]
        .add(weights * arrived_time[:, None])
    )
    weight_sum = jnp.zeros((local_events * blocks, 128), jnp.float32).at[arrived_place].add(weights)
    numerator = numerator.reshape(local_events, rows_all, local_cols)
    weight_sum = weight_sum.reshape(local_events, rows_all, local_cols)
    columns = tile_index * local_cols + jnp.arange(local_cols + 2 * 2, dtype=jnp.int32) - 2
    inside = ((columns >= 0) & (columns < tile_count * local_cols)).astype(jnp.float32)[
        None, None, :
    ]
    numer_wide = jnp.pad(numerator, ((0, 0), (0, 0), (2, 2)))
    sum_wide = jnp.pad(weight_sum, ((0, 0), (0, 0), (2, 2)))
    change = SMOOTH * numerator
    for sweep_index in range(SWEEPS - 1):
        widened = extended(change, (("tile", 2),), 2)
        change = sweep_once(widened, numer_wide, sum_wide, inside)[:, :, 2:-2]
    margin = extended(change, (("tile", 2),), 1)
    row_pos = jnp.arange(rows_all, dtype=jnp.float32)
    col_pos = (tile_index * local_cols + jnp.arange(local_cols, dtype=jnp.int32)).astype(
        jnp.float32
    )
    wave_speed = speed_field(margin, row_pos, col_pos, source_row, source_col)
    stacked = jnp.sum(valid_cells * wave_speed, axis=0)
    hit_count = jnp.sum(valid_cells, axis=0)
    stacked, hit_count = lax.psum((stacked, hit_count), "ev")
    row_share = rows_all // lax.axis_size("ev")
    row_start = lax.axis_index("ev") * row_share
    stacked = lax.dynamic_slice_in_dim(stacked, row_start, row_share, 0)
    hit_count = lax.dynamic_slice_in_dim(hit_count, row_start, row_share, 0)
    return stacked / (1.0 + hit_count)


def solution(mesh):
    placed = (
        P("tile", "ev", None),
        P("tile", "ev", None),
        P("tile", "ev", None),
        P("tile", "ev", None, None),
        P("tile", "ev"),
        P(),
        P("ev"),
        P("ev"),
        P("ev", None, "tile"),
    )
    return jax.shard_map(
        on_device, mesh=mesh, in_specs=placed, out_specs=P("ev", "tile"), check_vma=False
    )
```

profile of v0, /device:TPU:1, one launch (start us, length us, event | category | flops | bytes accessed | tf_op | source)
XLA Modules:
  0.0 1309.0 jit_solution(11485105753535993349)
XLA Ops:
  11.0 1.1 reduce-window.6
  13.2 1.9 scatter_fusion
  15.9 18.1 %all-to-all-start = ((f32[3,8,128]{2,0,1:T(4,128)}), f32[3,8,128]{2,0,1:T(4,128)S(1)}, u32[]{:S(2)}, u32[]{:S(2)}) async-start(f32[3,8,128]{2,0,1:T(4,128)} %copy.16), calls=%async_computation | async-start | bytes 32768 | tf_op jit(solution)/shard_map/all_to_all | solution.py:84
  34.1 13.7 %all-to-all-done = f32[3,8,128]{2,0,1:T(4,128)S(1)} async-done(((f32[3,8,128]{2,0,1:T(4,128)}), f32[3,8,128]{2,0,1:T(4,128)S(1)}, u32[]{:S(2)}, u32[]{:S(2)}) %all-to-all-start) | async-done | bytes 12320 | tf_op jit(solution)/shard_map/all_to_all | solution.py:84
  48.2 7.6 scatter_custom_fusion.1
  56.2 1.2 fusion.53
  57.3 3.3 collective-permute-start
  60.7 1.3 collective-permute-start.1
  62.0 7.8 scatter_custom_fusion.2
  69.8 1.5 reshape.289
  71.4 3.3 collective-permute-done
  74.7 47.5 %collective-permute-done.1 = f32[2,512,2]{2,1,0:T(8,128)} collective-permute-done((f32[2,512,2]{2,1,0:T(8,128)}, f32[2,512,2]{2,1,0:T(8,128)}, u32[]{:S(2)}, u32[]{:S(2)}) %collective-permute-start.1) | collective-permute-done | bytes 8224 | tf_op jit(solution)/shard_map/ppermute | solution.py:20
  122.2 1.8 pad_maximum_fusion
  124.0 0.9 subtract_multiply_fusion.2
  124.9 3.5 fusion.6
  128.6 1.3 collective-permute-start.2
  129.9 1.5 collective-permute-start.3
  131.8 14.2 %collective-permute-done.2 = f32[2,512,2]{2,1,0:T(8,128)S(1)} collective-permute-done((f32[2,512,2]{2,1,0:T(8,128)S(1)}, f32[2,512,2]{2,1,0:T(8,128)S(1)}, u32[]{:S(2)}, u32[]{:S(2)}) %collective-permute-start.2) | collective-permute-done | bytes 8224 | tf_op jit(solution)/shard_map/ppermute | solution.py:19
  146.0 8.5 collective-permute-done.3
  156.1 2.3 fusion.9
  158.5 36.5 %collective-permute-start.4 = (f32[2,512,2]{2,1,0:T(8,128)S(1)}, f32[2,512,2]{2,1,0:T(8,128)S(1)}, u32[]{:S(2)}, u32[]{:S(2)}) collective-permute-start(f32[2,512,2]{2,1,0:T(8,128)S(1)} %get-tuple-element.23), channel_id=1, source_target_pairs={{0,1},{1,2},{2,3},{3,4},{4,5},{5,6},{6,7},{8,9},{9,10},{10,11},{11... | collective-permute-start | bytes 24584 | tf_op jit(solution)/shard_map/ppermute | solution.py:19
  195.0 1.3 collective-permute-start.5
  196.7 9.0 collective-permute-done.4
  205.7 23.9 %collective-permute-done.5 = f32[2,512,2]{2,1,0:T(8,128)S(1)} collective-permute-done((f32[2,512,2]{2,1,0:T(8,128)S(1)}, f32[2,512,2]{2,1,0:T(8,128)S(1)}, u32[]{:S(2)}, u32[]{:S(2)}) %collective-permute-start.5) | collective-permute-done | bytes 8224 | tf_op jit(solution)/shard_map/ppermute | solution.py:20
  231.1 2.3 fusion.12
  233.7 49.8 %collective-permute-start.6 = (f32[2,512,1]{2,1,0:T(8,128)S(1)}, f32[2,512,1]{2,1,0:T(8,128)S(1)}, u32[]{:S(2)}, u32[]{:S(2)}) collective-permute-start(f32[2,512,1]{2,1,0:T(8,128)S(1)} %get-tuple-element.22), channel_id=1, source_target_pairs={{0,1},{1,2},{2,3},{3,4},{4,5},{5,6},{6,7},{8,9},{9,10},{10,11},{11... | collective-permute-start | bytes 12296 | tf_op jit(solution)/shard_map/ppermute | solution.py:19
  283.6 1.3 collective-permute-start.7
  285.3 27.4 %collective-permute-done.6 = f32[2,512,1]{2,1,0:T(8,128)S(1)} collective-permute-done((f32[2,512,1]{2,1,0:T(8,128)S(1)}, f32[2,512,1]{2,1,0:T(8,128)S(1)}, u32[]{:S(2)}, u32[]{:S(2)}) %collective-permute-start.6) | collective-permute-done | bytes 4128 | tf_op jit(solution)/shard_map/ppermute | solution.py:19
  312.7 23.3 %collective-permute-done.7 = f32[2,512,1]{2,1,0:T(8,128)S(1)} collective-permute-done((f32[2,512,1]{2,1,0:T(8,128)S(1)}, f32[2,512,1]{2,1,0:T(8,128)S(1)}, u32[]{:S(2)}, u32[]{:S(2)}) %collective-permute-start.7) | collective-permute-done | bytes 4128 | tf_op jit(solution)/shard_map/ppermute | solution.py:20
  336.7 3.0 fusion.26
  339.7 961.1 %all-reduce.12.cloned.1.call-done = (f32[512,256]{1,0:T(8,128)}, f32[512,256]{1,0:T(8,128)}) async-done(((f32[512,256]{1,0:T(8,128)}, f32[512,256]{1,0:T(8,128)}), (f32[512,256]{1,0:T(8,128)}, f32[512,256]{1,0:T(8,128)})) %all-reduce.12.cloned.1.call-update) | async-done | bytes 1048592 | tf_op jit(solution)/shard_map/psum | solution.py:122
  1300.8 1.3 add_divide_fusion
  (54 shorter events, 12.6 us)
Async XLA Ops:
  6.5 6.7 copy-start
  6.5 41.3 %copy-start.2 = (s32[64,128]{1,0:T(8,128)S(1)}, s32[64,128]{1,0:T(8,128)}, u32[]{:S(2)}) copy-start(s32[64,128]{1,0:T(8,128)} %param.16) | copy-start | bytes 98308
  15.9 31.9 %all-to-all-start = ((f32[3,8,128]{2,0,1:T(4,128)}), f32[3,8,128]{2,0,1:T(4,128)S(1)}, u32[]{:S(2)}, u32[]{:S(2)}) async-start(f32[3,8,128]{2,0,1:T(4,128)} %copy.16), calls=%async_computation | async-start | bytes 32768 | tf_op jit(solution)/shard_map/all_to_all | solution.py:84
  34.0 1266.8 %all-reduce.12.cloned.1.call-start = ((), (), s32[]{:S(2)}) async-start(), calls=%async_computation.1 | async-start | bytes 2097152 | tf_op jit(solution)/shard_map/psum | solution.py:122
  57.3 17.4 %collective-permute-start = (f32[2,512,2]{2,1,0:T(8,128)}, f32[2,512,2]{2,1,0:T(8,128)}, u32[]{:S(2)}, u32[]{:S(2)}) collective-permute-start(f32[2,512,2]{2,1,0:T(8,128)} %get-tuple-element.27), channel_id=1, source_target_pairs={{0,1},{1,2},{2,3},{3,4},{4,5},{5,6},{6,7},{8,9},{9,10},{10,11},{11... | collective-permute-start | bytes 24584 | tf_op jit(solution)/shard_map/ppermute | solution.py:19
  60.7 61.5 %collective-permute-start.1 = (f32[2,512,2]{2,1,0:T(8,128)}, f32[2,512,2]{2,1,0:T(8,128)}, u32[]{:S(2)}, u32[]{:S(2)}) collective-permute-start(f32[2,512,2]{2,1,0:T(8,128)} %get-tuple-element.28), channel_id=1, source_target_pairs={{1,0},{2,1},{3,2},{4,3},{5,4},{6,5},{7,6},{9,8},{10,9},{11,10},{12... | collective-permute-start | bytes 24584 | tf_op jit(solution)/shard_map/ppermute | solution.py:20
  128.4 3.0 copy-start.3
  128.6 17.4 %collective-permute-start.2 = (f32[2,512,2]{2,1,0:T(8,128)S(1)}, f32[2,512,2]{2,1,0:T(8,128)S(1)}, u32[]{:S(2)}, u32[]{:S(2)}) collective-permute-start(f32[2,512,2]{2,1,0:T(8,128)S(1)} %get-tuple-element.25), channel_id=1, source_target_pairs={{0,1},{1,2},{2,3},{3,4},{4,5},{5,6},{6,7},{8,9},{9,10},{10,11},{11... | collective-permute-start | bytes 24584 | tf_op jit(solution)/shard_map/ppermute | solution.py:19
  129.9 24.6 %collective-permute-start.3 = (f32[2,512,2]{2,1,0:T(8,128)S(1)}, f32[2,512,2]{2,1,0:T(8,128)S(1)}, u32[]{:S(2)}, u32[]{:S(2)}) collective-permute-start(f32[2,512,2]{2,1,0:T(8,128)S(1)} %get-tuple-element.26), channel_id=1, source_target_pairs={{1,0},{2,1},{3,2},{4,3},{5,4},{6,5},{7,6},{9,8},{10,9},{11,10},{12... | collective-permute-start | bytes 24584 | tf_op jit(solution)/shard_map/ppermute | solution.py:20
  158.5 47.2 %collective-permute-start.4 = (f32[2,512,2]{2,1,0:T(8,128)S(1)}, f32[2,512,2]{2,1,0:T(8,128)S(1)}, u32[]{:S(2)}, u32[]{:S(2)}) collective-permute-start(f32[2,512,2]{2,1,0:T(8,128)S(1)} %get-tuple-element.23), channel_id=1, source_target_pairs={{0,1},{1,2},{2,3},{3,4},{4,5},{5,6},{6,7},{8,9},{9,10},{10,11},{11... | collective-permute-start | bytes 24584 | tf_op jit(solution)/shard_map/ppermute | solution.py:19
  195.0 34.6 %collective-permute-start.5 = (f32[2,512,2]{2,1,0:T(8,128)S(1)}, f32[2,512,2]{2,1,0:T(8,128)S(1)}, u32[]{:S(2)}, u32[]{:S(2)}) collective-permute-start(f32[2,512,2]{2,1,0:T(8,128)S(1)} %get-tuple-element.24), channel_id=1, source_target_pairs={{1,0},{2,1},{3,2},{4,3},{5,4},{6,5},{7,6},{9,8},{10,9},{11,10},{12... | collective-permute-start | bytes 24584 | tf_op jit(solution)/shard_map/ppermute | solution.py:20
  233.4 51.5 %copy-start.4 = (f32[2]{0:T(128)S(1)}, f32[2]{0:T(128)}, u32[]{:S(2)}) copy-start(f32[2]{0:T(128)} %param.18) | copy-start | bytes 28
  233.7 79.0 %collective-permute-start.6 = (f32[2,512,1]{2,1,0:T(8,128)S(1)}, f32[2,512,1]{2,1,0:T(8,128)S(1)}, u32[]{:S(2)}, u32[]{:S(2)}) collective-permute-start(f32[2,512,1]{2,1,0:T(8,128)S(1)} %get-tuple-element.22), channel_id=1, source_target_pairs={{0,1},{1,2},{2,3},{3,4},{4,5},{5,6},{6,7},{8,9},{9,10},{10,11},{11... | collective-permute-start | bytes 12296 | tf_op jit(solution)/shard_map/ppermute | solution.py:19
  283.6 52.5 %collective-permute-start.7 = (f32[2,512,1]{2,1,0:T(8,128)S(1)}, f32[2,512,1]{2,1,0:T(8,128)S(1)}, u32[]{:S(2)}, u32[]{:S(2)}) collective-permute-start(f32[2,512,1]{2,1,0:T(8,128)S(1)} %get-tuple-element.21), channel_id=1, source_target_pairs={{1,0},{2,1},{3,2},{4,3},{5,4},{6,5},{7,6},{9,8},{10,9},{11,10},{12... | collective-permute-start | bytes 12296 | tf_op jit(solution)/shard_map/ppermute | solution.py:20
  285.3 51.4 %copy-start.1 = (f32[2,512,256]{2,1,0:T(8,128)S(1)}, f32[2,512,256]{2,1,0:T(8,128)}, u32[]{:S(2)}) copy-start(f32[2,512,256]{2,1,0:T(8,128)} %param.19) | copy-start | bytes 3145732
Sparse Core Ops, SparseCore 0:
  339.8 960.9 all-reduce.11
where the time goes:
time: 1310 us
  waiting for transfers between devices  1130 us (86%)
  starting transfers between devices  114 us (9%)
  other arithmetic  38.4 us (3%)
  between operations  13.7 us (1%)
    psum x1, waiting for transfers between devices, on_device(): stacked, hit_count = lax.psum((stacked, hit_count), 'ev')  961 us
    ppermute x4, waiting for transfers between devices, extended(): after = lax.ppermute(initial, axis, down)  103 us
    ppermute x4, starting transfers between devices, extended(): before = lax.ppermute(last, axis, up)  91 us
    ppermute x4, waiting for transfers between devices, extended(): before = lax.ppermute(last, axis, up)  54 us
  transfers between devices with their start and end apart: 10, of which 10 were waited for; matrix products, arithmetic and copies ran while one was open for 1% of the time, Pallas kernels for 0%

commit v1 on v0

v1 whole, which is shorter than its diff:
```python
import functools

import jax
import jax.numpy as jnp
import numpy as np
from jax import lax
from jax.experimental import pallas as pl
from jax.experimental.pallas import tpu as pltpu
from jax.sharding import Mesh
from jax.sharding import PartitionSpec as P

SWEEPS = 4
SMOOTH = 0.024

YS, ZS, CS, XS, WS = 4, 8, 2, 4, 2
EV, TILE = ("y", "z", "c"), ("x", "w")
LISTS = XS * WS

EVENTS, SLOTS, ROWS, COLS, LANES = 2, 256, 512, 256, 128
KERN = 64
SHARE = ROWS // (YS * ZS * CS)
PAD = 8
TILES = 3
CHUNK = 64


def pack(times, kernels, blocks, dests, counts, out):
    lane = lax.broadcasted_iota(jnp.int32, (1, LANES), 1)
    for e in range(EVENTS):
        for h in range(2):
            part = slice(h * LANES, (h + 1) * LANES)
            live = lane + h * LANES < counts[0, e]
            k = 2 * e + h
            out[0, k : k + 1, :] = times[0, e : e + 1, part]
            out[0, 4 + k : 5 + k, :] = jnp.where(live, kernels[0, e : e + 1, part], -1).astype(jnp.float32)
            out[0, 8 + k : 9 + k, :] = blocks[0, e : e + 1, part].astype(jnp.float32)
            out[0, 12 + k : 13 + k, :] = dests[e : e + 1, part].astype(jnp.float32)
    for p in range(1, LISTS):
        out[p] = out[0]


def gather_maps(arrived, table, tile, onehot, cells, weights, numer):
    f32, bf16 = jnp.float32, jnp.bfloat16
    table_t = jnp.transpose(table[...].astype(f32)).astype(bf16)
    pick = lax.broadcasted_iota(jnp.int32, (KERN, SLOTS), 0)
    row_of = lax.broadcasted_iota(jnp.int32, (ROWS, SLOTS), 0)
    lane = lax.broadcasted_iota(jnp.int32, (1, LANES), 1)

    for e in range(EVENTS):

        def one_list(t, carry, e=e):
            def both(k):
                k = k + 2 * e
                return jnp.concatenate([arrived[t, k : k + 1, :], arrived[t, k + 1 : k + 2, :]], axis=1)

            time = both(0)
            kernel = both(4).astype(jnp.int32)
            block = both(8).astype(jnp.int32)
            dest = both(12).astype(jnp.int32)
            seg = dest * 2 + (block & 1) - 2 * tile
            row = block >> 1
            at = pl.ds(pl.multiple_of(t * SLOTS, SLOTS), SLOTS)
            onehot[:, at] = jnp.where(row_of == row, 1.0, 0.0).astype(bf16)
            picked = jnp.where(pick == kernel, 1.0, 0.0).astype(bf16)
            w = jnp.dot(table_t, picked, preferred_element_type=f32) * (1.0 / 256.0)
            v = w * time
            v_hi = v.astype(bf16).astype(f32)
            v_lo = v - v_hi
            for k, part in enumerate((w, v_hi, v_lo)):
                for h in range(2):
                    cells[pl.ds((2 * k + h) * LANES, LANES), at] = jnp.where(seg == h, part, 0.0).astype(bf16)
            right, left = seg == 2, seg == -1
            border = [jnp.where(right, part[:8], 0.0) for part in (w, v_hi, v_lo)]
            border.append(jnp.zeros((80, SLOTS), f32))
            border += [jnp.where(left, part[LANES - 8 :], 0.0) for part in (v_lo, v_hi, w)]
            cells[pl.ds(6 * LANES, LANES), at] = jnp.concatenate(border, axis=0).astype(bf16)
            return carry

        lax.fori_loop(0, LISTS, one_list, 0)

        for r in range(0, ROWS, 256):
            sums = lax.dot_general(
                onehot[r : r + 256, :], cells[...], (((1,), (1,)), ((), ())), preferred_element_type=f32
            )
            for h in range(2):
                cut = lambda k: sums[:, (2 * k + h) * LANES : (2 * k + h + 1) * LANES]
                weights[TILES * e + h, r : r + 256, :] = cut(0)
                numer[TILES * e + h, r : r + 256, :] = cut(1) + cut(2)
            edge = sums[:, 6 * LANES :]
            beside = (lane < 8) | (lane >= LANES - 8)
            right = pltpu.roll(edge, LANES - 8, 1) + pltpu.roll(edge, LANES - 16, 1)
            left = pltpu.roll(edge, 8, 1) + pltpu.roll(edge, 16, 1)
            weights[TILES * e + 2, r : r + 256, :] = jnp.where(beside, edge, 0.0)
            numer[TILES * e + 2, r : r + 256, :] = jnp.where(
                lane < 8, right, jnp.where(lane >= LANES - 8, left, 0.0)
            )


def beside(tiles, lane):
    up = [pltpu.roll(x, 1, 1) for x in tiles]
    down = [pltpu.roll(x, LANES - 1, 1) for x in tiles]
    n = len(tiles)
    left = [jnp.where(lane == 0, up[(j + n - 1) % n], up[j]) for j in range(n)]
    right = [jnp.where(lane == LANES - 1, down[(j + 1) % n], down[j]) for j in range(n)]
    return left, right


def laplace_of(buf, first, r0, lane):
    near = [buf[first + j, pl.ds(r0 + PAD, CHUNK), :] for j in range(TILES)]
    left, right = beside(near, lane)
    out = []
    for j in range(TILES):
        above = buf[first + j, pl.ds(r0 + PAD - 1, CHUNK), :]
        below = buf[first + j, pl.ds(r0 + PAD + 1, CHUNK), :]
        out.append((above + below) + (left[j] + right[j]) - 4.0 * near[j])
    return out


def work(
    arrived, table, source_row, source_col, valid_hbm, send, keep,
    onehot, cells, weights, numer, change, curve, valid, arrival,
):
    tile = lax.axis_index("x") * WS + lax.axis_index("w")
    core = lax.axis_index("c")
    copy = pltpu.make_async_copy(valid_hbm, valid, arrival)
    copy.start()
    gather_maps(arrived, table, tile, onehot, cells, weights, numer)

    lane = lax.broadcasted_iota(jnp.int32, (1, LANES), 1)
    half = LANES // 2
    inside = jnp.where(((tile == 0) & (lane >= half)) | ((tile == LISTS - 1) & (lane < half)), 0.0, 1.0)
    empty = jnp.zeros((PAD, LANES), jnp.float32)
    for k in range(EVENTS * TILES):
        for buf in (change, curve):
            buf[k, 0:PAD, :] = empty
            buf[k, ROWS + PAD : ROWS + 2 * PAD, :] = empty
    spans = ROWS // CHUNK

    def first_sweep(i, carry):
        r0 = pl.multiple_of(i * CHUNK, CHUNK)
        for k in range(EVENTS * TILES):
            change[k, pl.ds(r0 + PAD, CHUNK), :] = SMOOTH * numer[k, pl.ds(r0, CHUNK), :]
        return carry

    lax.fori_loop(0, spans, first_sweep, 0)

    def curve_pass(i, carry):
        r0 = pl.multiple_of(i * CHUNK, CHUNK)
        for e in range(EVENTS):
            laps = laplace_of(change, TILES * e, r0, lane)
            laps[2] = laps[2] * inside
            for j in range(TILES):
                curve[TILES * e + j, pl.ds(r0 + PAD, CHUNK), :] = laps[j]
        return carry

    def update_pass(i, carry):
        r0 = pl.multiple_of(i * CHUNK, CHUNK)
        for e in range(EVENTS):
            bends = laplace_of(curve, TILES * e, r0, lane)
            for j in range(TILES):
                k = TILES * e + j
                at = pl.ds(r0 + PAD, CHUNK)
                old = change[k, at, :]
                pull = weights[k, pl.ds(r0, CHUNK), :] * old - numer[k, pl.ds(r0, CHUNK), :]
                new = old - SMOOTH * (bends[j] + pull)
                change[k, at, :] = new * inside if j == 2 else new
        return carry

    def sweep(s, carry):
        lax.fori_loop(0, spans, curve_pass, 0)
        lax.fori_loop(0, spans, update_pass, 0)
        return carry

    lax.fori_loop(0, SWEEPS - 1, sweep, 0)
    copy.wait()

    column = lax.broadcasted_iota(jnp.int32, (1, LANES), 1) + tile * COLS
    line = lax.broadcasted_iota(jnp.int32, (SHARE, 1), 0)

    def stack(out, core_of):
        def one_share(g, carry):
            r0 = pl.multiple_of(g * (CS * SHARE) + core_of * SHARE, SHARE)
            total = [jnp.zeros((SHARE, LANES), jnp.float32) for h in range(2)]
            hits = [jnp.zeros((SHARE, LANES), jnp.float32) for h in range(2)]
            for e in range(EVENTS):
                near = [change[TILES * e + j, pl.ds(r0 + PAD, SHARE), :] for j in range(TILES)]
                left, right = beside(near, lane)
                off_row = (line + r0).astype(jnp.float32) - source_row[e]
                for h in range(2):
                    above = change[TILES * e + h, pl.ds(r0 + PAD - 1, SHARE), :]
                    below = change[TILES * e + h, pl.ds(r0 + PAD + 1, SHARE), :]
                    off_col = (column + h * LANES).astype(jnp.float32) - source_col[e]
                    inverse = lax.rsqrt(off_row * off_row + off_col * off_col)
                    along_row = off_row * inverse + 0.5 * (below - above)
                    along_col = off_col * inverse + 0.5 * (right[h] - left[h])
                    speed = jnp.sqrt(along_row * along_row + along_col * along_col)
                    cell = valid[e, pl.ds(r0, SHARE), h * LANES : (h + 1) * LANES]
                    total[h] = total[h] + cell * speed
                    hits[h] = hits[h] + cell
            for h in range(2):
                part = slice(h * LANES, (h + 1) * LANES)
                out[g, 0, :, part] = total[h]
                out[g, 1, :, part] = hits[h]
            return carry

        lax.fori_loop(0, YS * ZS, one_share, 0)

    stack(send, 1 - core)
    stack(keep, core)


def maps_of(arrived, table, source_row, source_col, valid):
    f32 = jnp.float32
    shares = jax.ShapeDtypeStruct((YS * ZS, 2, SHARE, COLS), f32)
    vmem, smem = pl.BlockSpec(memory_space=pltpu.VMEM), pl.BlockSpec(memory_space=pltpu.SMEM)
    wide = pltpu.VMEM((EVENTS * TILES, ROWS, LANES), f32)
    padded = pltpu.VMEM((EVENTS * TILES, ROWS + 2 * PAD, LANES), f32)
    return pl.pallas_call(
        work,
        out_shape=(shares, shares),
        in_specs=[vmem, vmem, smem, smem, pl.BlockSpec(memory_space=pl.ANY)],
        out_specs=(vmem, vmem),
        scratch_shapes=[
            pltpu.VMEM((ROWS, LISTS * SLOTS), jnp.bfloat16),
            pltpu.VMEM((7 * LANES, LISTS * SLOTS), jnp.bfloat16),
            wide, wide, padded, padded,
            pltpu.VMEM((EVENTS, ROWS, COLS), f32),
            pltpu.SemaphoreType.DMA,
        ],
        compiler_params=pltpu.CompilerParams(vmem_limit_bytes=40 * 1024 * 1024),
        name="maps",
    )(arrived, table, source_row, source_col, valid)


def packed(times, kernels, blocks, dests, counts):
    vmem, smem = pl.BlockSpec(memory_space=pltpu.VMEM), pl.BlockSpec(memory_space=pltpu.SMEM)
    return pl.pallas_call(
        pack,
        out_shape=jax.ShapeDtypeStruct((LISTS, 16, LANES), jnp.float32),
        in_specs=[vmem, vmem, vmem, vmem, smem],
        out_specs=vmem,
        name="pack",
    )(times, kernels, blocks, dests, counts)


def on_device(times, kernels, blocks, dests, counts, table, source_row, source_col, valid):
    outgoing = packed(times, kernels, blocks, dests.reshape(EVENTS, SLOTS), counts)
    arrived = lax.all_to_all(outgoing, TILE, 0, 0, tiled=True)
    send, keep = maps_of(arrived, table, source_row, source_col, valid)
    both = keep + lax.ppermute(send, "c", [(0, 1), (1, 0)])
    both = both.reshape(YS, ZS, 2, SHARE, COLS)
    both = jnp.sum(lax.all_to_all(both, "y", 0, 0, tiled=True), axis=0)
    both = jnp.sum(lax.all_to_all(both, "z", 0, 0, tiled=True), axis=0)
    return both[0] / (1.0 + both[1])


def solution(mesh):
    split = Mesh(np.asarray(mesh.devices).reshape(YS, ZS, CS, XS, WS), EV + TILE)
    placed = (
        P(TILE, EV, None),
        P(TILE, EV, None),
        P(TILE, EV, None),
        P(TILE, EV, None, None),
        P(TILE, EV),
        P(),
        P(EV),
        P(EV),
        P(EV, None, TILE),
    )
    return jax.shard_map(on_device, mesh=split, in_specs=placed, out_specs=P(EV, TILE), check_vma=False)
```

time: 1310 us -> 95.7 us (0.07)
  the two profiles are of different devices: /device:TPU:1 before, /device:TPU:2 now
where the time goes in v1:
time: 95.7 us; the launch traced here: 95.3 us
  blocking collectives  62.1 us (65%)
  Pallas kernels  26.1 us (27%)
  local copies, waits for them, and re-layouts  2.49 us (3%)
  starting transfers between devices  1.92 us (2%)
  waiting for transfers between devices  1.88 us (2%)
    all_to_all x1, blocking collectives, on_device(): arrived = lax.all_to_all(outgoing, TILE, 0, 0, tiled=True)  31.8 us
    pallas_call x1, Pallas kernels, maps_of(): pl.pallas_call(work, out_shape=(shares, shares), in_specs=[vmem, vmem, sm...  24.7 us
    all_to_all x1, blocking collectives, on_device(): both = jnp.sum(lax.all_to_all(both, 'z', 0, 0, tiled=True), axis=0)  16.3 us
    all_to_all x1, blocking collectives, on_device(): both = jnp.sum(lax.all_to_all(both, 'y', 0, 0, tiled=True), axis=0)  14 us
    unnamed x9, local copies, waits for them, and re-layouts  2.49 us
    ppermute x1, starting transfers between devices, on_device(): both = keep + lax.ppermute(send, 'c', [(0, 1), (1, 0)])  1.92 us
  transfers between devices with their start and end apart: 1, of which 1 were waited for; matrix products, arithmetic and copies ran while one was open for 0% of the time, Pallas kernels for 0%

profile of v1, /device:TPU:2, one launch (start us, length us, event | category | flops | bytes accessed | tf_op | source)
XLA Modules:
  0.0 95.3 jit_solution(1097811034483623455)
XLA Ops:
  0.0 1.3 %copy.12 = s32[1,2,256,1]{2,1,3,0:T(2,128)} copy(s32[1,2,256,1]{2,3,1,0:T(1,128)} %param.12) | data formatting | bytes 4096
  1.3 1.4 %pack.1 = f32[8,16,128]{2,1,0:T(8,128)} custom-call(f32[1,2,256]{2,1,0:T(2,128)} %times.1, s32[1,2,256]{2,1,0:T(2,128)} %kernels.1, s32[1,2,256]{2,1,0:T(2,128)} %blocks.1, s32[2,256]{1,0:T(2,128)} %bitcast.7, s32[1,2]{1,0:T(1,128)} %counts.1), custom_call_target="tpu_custom_call" | custom-call | tf_op jit(solution)/shard_map/pack/pallas_call | solution.py:237
  2.7 0.0 copy-start.1
  2.7 0.0 copy-start.2
  2.7 0.0 copy-start.3
  2.7 31.8 %all_to_all.15.arrived = f32[8,16,128]{2,1,0:T(8,128)S(1)} all-to-all(f32[8,16,128]{2,1,0:T(8,128)} %pack.1), channel_id=1, replica_groups=mesh['y'=4,'z'=8,'c'=2,'x'=4,'w'=2] {'x','w'}, dimensions={0} | all-to-all | bytes 131072 | tf_op jit(solution)/shard_map/all_to_all | solution.py:248
  34.5 0.0 copy-done.1
  34.5 0.0 copy-done.2
  34.5 0.0 copy-done.3
  34.5 0.0 copy-start
  34.5 1.2 %copy-done = f32[2,512,256]{2,1,0:T(8,128)S(1)} copy-done((f32[2,512,256]{2,1,0:T(8,128)S(1)}, f32[2,512,256]{2,1,0:T(8,128)}, u32[]{:S(2)}) %copy-start) | copy-done | bytes 1048600
  35.8 24.7 %maps.1 = (f32[32,2,8,256]{3,2,1,0:T(8,128)S(1)}, f32[32,2,8,256]{3,2,1,0:T(8,128)S(1)}) custom-call(f32[8,16,128]{2,1,0:T(8,128)S(1)} %all_to_all.15.arrived, s32[64,128]{1,0:T(8,128)S(1)} %copy-done.1, f32[2]{0:T(128)S(1)} %copy-done.2, f32[2]{0:T(128)S(1)} %copy-done.3, f32[2,512,256]{2,1,0:T(8,128)S(1)} %copy-done), custom_call_target="tpu_custom_call" | custom-call | tf_op jit(solution)/shard_map/maps/pallas_call | solution.py:218
  60.4 1.9 %collective-permute-start = (f32[32,2,8,256]{3,2,1,0:T(8,128)S(1)}, f32[32,2,8,256]{3,2,1,0:T(8,128)S(1)}, u32[]{:S(2)}, u32[]{:S(2)}) collective-permute-start(f32[32,2,8,256]{3,2,1,0:T(8,128)S(1)} %get-tuple-element.8), channel_id=1, source_target_pairs={{0,8},{8,0},{1,9},{9,1},{2,10},{10,2},{3,11},{11,3},{4,12},{12,4},... | collective-permute-start | bytes 1572872 | tf_op jit(solution)/shard_map/ppermute | solution.py:250
  62.4 1.9 %collective-permute-done = f32[32,2,8,256]{3,2,1,0:T(8,128)S(1)} collective-permute-done((f32[32,2,8,256]{3,2,1,0:T(8,128)S(1)}, f32[32,2,8,256]{3,2,1,0:T(8,128)S(1)}, u32[]{:S(2)}, u32[]{:S(2)}) %collective-permute-start) | collective-permute-done | bytes 524320 | tf_op jit(solution)/shard_map/ppermute | solution.py:250
  64.2 0.1 add.10
  64.3 14.0 %all_to_all.16 = f32[4,8,2,8,256]{4,3,2,1,0:T(8,128)S(1)} all-to-all(f32[4,8,2,8,256]{4,3,2,1,0:T(8,128)S(1)} %bitcast.6), channel_id=1, replica_groups=mesh['y'=4,'z'=8,'c'=2,'x'=4,'w'=2] {'y'}, dimensions={0} | all-to-all | bytes 1048576 | tf_op jit(solution)/shard_map/all_to_all | solution.py:252
  78.4 16.3 %all_to_all.17 = f32[8,2,8,256]{3,2,1,0:T(8,128)S(1)} all-to-all(f32[8,2,8,256]{3,2,1,0:T(8,128)S(1)} %reduce_sum.18), channel_id=1, replica_groups=mesh['y'=4,'z'=8,'c'=2,'x'=4,'w'=2] {'z'}, dimensions={0} | all-to-all | bytes 262144 | tf_op jit(solution)/shard_map/all_to_all | solution.py:253
  94.7 0.6 fusion.1
  (2 shorter events, 0.1 us)
Async XLA Ops:
  2.7 31.8 %copy-start.1 = (s32[64,128]{1,0:T(8,128)S(1)}, s32[64,128]{1,0:T(8,128)}, u32[]{:S(2)}) copy-start(s32[64,128]{1,0:T(8,128)} %table.1) | copy-start | bytes 98308
  2.7 31.8 %copy-start.2 = (f32[2]{0:T(128)S(1)}, f32[2]{0:T(128)}, u32[]{:S(2)}) copy-start(f32[2]{0:T(128)} %source_row.1) | copy-start | bytes 28
  2.7 31.8 %copy-start.3 = (f32[2]{0:T(128)S(1)}, f32[2]{0:T(128)}, u32[]{:S(2)}) copy-start(f32[2]{0:T(128)} %source_col.1) | copy-start | bytes 28
  34.5 1.2 %copy-start = (f32[2,512,256]{2,1,0:T(8,128)S(1)}, f32[2,512,256]{2,1,0:T(8,128)}, u32[]{:S(2)}) copy-start(f32[2,512,256]{2,1,0:T(8,128)} %valid_hbm.1) | copy-start | bytes 3145732
  60.4 3.8 %collective-permute-start = (f32[32,2,8,256]{3,2,1,0:T(8,128)S(1)}, f32[32,2,8,256]{3,2,1,0:T(8,128)S(1)}, u32[]{:S(2)}, u32[]{:S(2)}) collective-permute-start(f32[32,2,8,256]{3,2,1,0:T(8,128)S(1)} %get-tuple-element.8), channel_id=1, source_target_pairs={{0,8},{8,0},{1,9},{9,1},{2,10},{10,2},{3,11},{11,3},{4,12},{12,4},... | collective-permute-start | bytes 1572872 | tf_op jit(solution)/shard_map/ppermute | solution.py:250

commit v2 on v1

v2 whole, which is shorter than its diff:
```python
import functools

import jax
import jax.numpy as jnp
import numpy as np
from jax import lax
from jax.experimental import pallas as pl
from jax.experimental.pallas import tpu as pltpu
from jax.sharding import Mesh
from jax.sharding import PartitionSpec as P

SWEEPS = 4
SMOOTH = 0.024

YS, ZS, CS, XS, WS = 4, 8, 2, 4, 2
EV, TILE = ("y", "z", "c"), ("x", "w")
LISTS = XS * WS
UNROLL = 8

EVENTS, SLOTS, ROWS, COLS, LANES = 2, 256, 512, 256, 128
KERN = 64
SHARE = ROWS // (YS * ZS * CS)
PAD = 8
EDGE = 8
SPAN = COLS + 2 * EDGE
LINES = ROWS // LANES
BLOCK = 32


def pack(times, kernels, blocks, dests, counts, out):
    lane = lax.broadcasted_iota(jnp.int32, (1, LANES), 1)
    for e in range(EVENTS):
        for h in range(2):
            part = slice(h * LANES, (h + 1) * LANES)
            live = lane + h * LANES < counts[0, e]
            k = 2 * e + h
            out[0, k : k + 1, :] = times[0, e : e + 1, part]
            out[0, 4 + k : 5 + k, :] = jnp.where(live, kernels[0, e : e + 1, part], -1).astype(jnp.float32)
            out[0, 8 + k : 9 + k, :] = blocks[0, e : e + 1, part].astype(jnp.float32)
            out[0, 12 + k : 13 + k, :] = dests[e, :, part].astype(jnp.float32)
    for p in range(1, LISTS):
        out[p] = out[0]


def gather_maps(arrived, table, tile, onehot, cells, weights, numer, change):
    f32, bf16 = jnp.float32, jnp.bfloat16
    columns = jnp.transpose(table[...].astype(f32)) * (1.0 / 256.0)
    none = jnp.zeros((LANES, KERN), f32)
    by_segment = jnp.concatenate(
        [
            jnp.concatenate([columns[LANES - EDGE :]] + [none[:EDGE]] * 3, axis=1),
            jnp.concatenate([none, columns, none, none], axis=1),
            jnp.concatenate([none, none, columns, none], axis=1),
            jnp.concatenate([none[:EDGE]] * 3 + [columns[:EDGE]], axis=1),
        ],
        axis=0,
    ).astype(bf16)
    pick = lax.broadcasted_iota(jnp.int32, (4 * KERN, SLOTS), 0)
    row_of = lax.broadcasted_iota(jnp.int32, (ROWS, SLOTS), 0)

    for e in range(EVENTS):

        def one_list(t, carry, e=e):
            def both(k):
                k = k + 2 * e
                return jnp.concatenate([arrived[t, k : k + 1, :], arrived[t, k + 1 : k + 2, :]], axis=1)

            time = both(0)
            kernel = both(4).astype(jnp.int32)
            block = both(8).astype(jnp.int32)
            dest = both(12).astype(jnp.int32)
            seg = dest * 2 + (block & 1) - 2 * tile + 1
            row = block >> 1
            place = (row & (LINES - 1)) * LANES + row // LINES
            choice = jnp.where((kernel >= 0) & (seg >= 0) & (seg < 4), seg * KERN + kernel, -1)
            at = pl.ds(pl.multiple_of(t * SLOTS, SLOTS), SLOTS)
            onehot[:, at] = jnp.where(row_of == place, 1.0, 0.0).astype(bf16)
            picked = jnp.where(pick == choice, 1.0, 0.0).astype(bf16)
            w = jnp.dot(by_segment, picked, preferred_element_type=f32)
            v = w * time
            v_hi = v.astype(bf16)
            cells[0:SPAN, at] = w.astype(bf16)
            cells[SPAN : 2 * SPAN, at] = v_hi
            cells[2 * SPAN : 3 * SPAN, at] = (v - v_hi.astype(f32)).astype(bf16)
            return carry

        lax.fori_loop(0, LISTS, one_list, 0, unroll=UNROLL)

        def total(k):
            return lax.dot_general(
                cells[k * SPAN : (k + 1) * SPAN, :], onehot[...], (((1,), (1,)), ((), ())), preferred_element_type=f32
            )

        weight = total(0)
        number = total(1) + total(2)
        for t in range(LINES):
            part = slice(t * LANES, (t + 1) * LANES)
            weights[e, t] = weight[:, part]
            numer[e, t] = number[:, part]
            change[e, t, PAD : PAD + SPAN, :] = SMOOTH * number[:, part]


def beside(tiles, lane):
    first = jnp.where(lane == 0, 0.0, pltpu.roll(tiles[-1], 1, 1))
    last = jnp.where(lane == LANES - 1, 0.0, pltpu.roll(tiles[0], LANES - 1, 1))
    return [first] + tiles[:-1], tiles[1:] + [last]


def laplace_of(buf, e, p, size, lane):
    near = [buf[e, t, PAD + p : PAD + p + size, :] for t in range(LINES)]
    above, below = beside(near, lane)
    out = []
    for t in range(LINES):
        left = buf[e, t, PAD + p - 1 : PAD + p - 1 + size, :]
        right = buf[e, t, PAD + p + 1 : PAD + p + 1 + size, :]
        out.append((left + right) + (above[t] + below[t]) - 4.0 * near[t])
    return out


def work(
    arrived, table, source_row, source_col, valid_hbm, send, keep,
    onehot, cells, weights, numer, change, curve, valid, stacked, arrivals,
):
    f32 = jnp.float32
    tile = lax.axis_index("x") * WS + lax.axis_index("w")
    core = lax.axis_index("c")
    copies = [
        pltpu.make_async_copy(
            valid_hbm.at[e, :, h * LANES : (h + 1) * LANES], valid.at[e, h], arrivals.at[2 * e + h]
        )
        for e in range(EVENTS)
        for h in range(2)
    ]
    for copy in copies:
        copy.start()
    empty = jnp.zeros((PAD, LANES), f32)
    for buf in (change, curve):
        for e in range(EVENTS):
            for t in range(LINES):
                buf[e, t, 0:PAD, :] = empty
                buf[e, t, PAD + SPAN :, :] = empty
    gather_maps(arrived, table, tile, onehot, cells, weights, numer, change)

    lane = lax.broadcasted_iota(jnp.int32, (1, LANES), 1)
    parts = [(p, min(BLOCK, SPAN - p)) for p in range(0, SPAN, BLOCK)]

    def outside(buf, e):
        @pl.when(tile == 0)
        def _():
            for t in range(LINES):
                buf[e, t, PAD : PAD + EDGE, :] = empty

        @pl.when(tile == LISTS - 1)
        def _():
            for t in range(LINES):
                buf[e, t, PAD + SPAN - EDGE : PAD + SPAN, :] = empty

    def curve_pass(e, carry):
        for p, size in parts:
            for t, lap in enumerate(laplace_of(change, e, p, size, lane)):
                curve[e, t, PAD + p : PAD + p + size, :] = lap
        outside(curve, e)
        return carry

    def update_pass(e, carry):
        for p, size in parts:
            for t, bend in enumerate(laplace_of(curve, e, p, size, lane)):
                old = change[e, t, PAD + p : PAD + p + size, :]
                pull = weights[e, t, p : p + size, :] * old - numer[e, t, p : p + size, :]
                change[e, t, PAD + p : PAD + p + size, :] = old - SMOOTH * (bend + pull)
        outside(change, e)
        return carry

    def sweep(s, carry):
        lax.fori_loop(0, EVENTS, curve_pass, 0)
        lax.fori_loop(0, EVENTS, update_pass, 0)
        return carry

    lax.fori_loop(0, SWEEPS - 1, sweep, 0)
    for copy in copies:
        copy.wait()

    lines = lax.broadcasted_iota(jnp.int32, (1, LANES), 1) * LINES
    column = lax.broadcasted_iota(jnp.int32, (LANES, 1), 0) + tile * COLS

    def stack(h, carry):
        p = pl.multiple_of(PAD + EDGE + h * LANES, 8)
        totals = [None] * LINES
        for e in range(EVENTS):
            near = [change[e, t, pl.ds(p, LANES), :] for t in range(LINES)]
            above, below = beside(near, lane)
            off_col = (column + h * LANES).astype(f32) - source_col[e]
            for t in range(LINES):
                left = change[e, t, pl.ds(p - 1, LANES), :]
                right = change[e, t, pl.ds(p + 1, LANES), :]
                off_row = (lines + t).astype(f32) - source_row[e]
                inverse = lax.rsqrt(off_row * off_row + off_col * off_col)
                along_row = off_row * inverse + 0.5 * (below[t] - above[t])
                along_col = off_col * inverse + 0.5 * (right - left)
                speed = jnp.sqrt(along_row * along_row + along_col * along_col)
                term = valid[e, h, pl.ds(t, LANES, stride=LINES), :] * jnp.transpose(speed)
                totals[t] = term if e == 0 else totals[t] + term
        for t in range(LINES):
            stacked[h, pl.ds(t, LANES, stride=LINES), :] = totals[t]
        return carry

    lax.fori_loop(0, 2, stack, 0)

    def deal(out, core_of):
        def one_share(g, carry):
            at = pl.ds(pl.multiple_of(g * (CS * SHARE) + core_of * SHARE, SHARE), SHARE)
            for h in range(2):
                part = slice(h * LANES, (h + 1) * LANES)
                out[g, 0, :, part] = stacked[h, at, :]
                out[g, 1, :, part] = valid[0, h, at, :] + valid[1, h, at, :]
            return carry

        lax.fori_loop(0, YS * ZS, one_share, 0, unroll=8)

    deal(send, 1 - core)
    deal(keep, core)


def maps_of(arrived, table, source_row, source_col, valid):
    f32 = jnp.float32
    shares = jax.ShapeDtypeStruct((YS * ZS, 2, SHARE, COLS), f32)
    vmem, smem = pl.BlockSpec(memory_space=pltpu.VMEM), pl.BlockSpec(memory_space=pltpu.SMEM)
    wide = pltpu.VMEM((EVENTS, LINES, SPAN, LANES), f32)
    padded = pltpu.VMEM((EVENTS, LINES, SPAN + 2 * PAD, LANES), f32)
    return pl.pallas_call(
        work,
        out_shape=(shares, shares),
        in_specs=[vmem, vmem, smem, smem, pl.BlockSpec(memory_space=pltpu.HBM)],
        out_specs=(vmem, vmem),
        scratch_shapes=[
            pltpu.VMEM((ROWS, LISTS * SLOTS), jnp.bfloat16),
            pltpu.VMEM((3 * SPAN, LISTS * SLOTS), jnp.bfloat16),
            wide, wide, padded, padded,
            pltpu.VMEM((EVENTS, 2, ROWS, LANES), f32),
            pltpu.VMEM((2, ROWS, LANES), f32),
            pltpu.SemaphoreType.DMA((2 * EVENTS,)),
        ],
        compiler_params=pltpu.CompilerParams(vmem_limit_bytes=40 * 1024 * 1024),
        name="maps",
    )(arrived, table, source_row, source_col, valid)


def packed(times, kernels, blocks, dests, counts):
    vmem, smem = pl.BlockSpec(memory_space=pltpu.VMEM), pl.BlockSpec(memory_space=pltpu.SMEM)
    return pl.pallas_call(
        pack,
        out_shape=jax.ShapeDtypeStruct((LISTS, 16, LANES), jnp.float32),
        in_specs=[vmem, vmem, vmem, vmem, smem],
        out_specs=vmem,
        name="pack",
    )(times, kernels, blocks, dests, counts)


def on_device(times, kernels, blocks, dests, counts, table, source_row, source_col, valid):
    outgoing = packed(times, kernels, blocks, dests.reshape(EVENTS, 1, SLOTS), counts)
    arrived = lax.all_to_all(outgoing, TILE, 0, 0, tiled=True)
    send, keep = maps_of(arrived, table, source_row, source_col, valid)
    both = keep + lax.ppermute(send, "c", [(0, 1), (1, 0)])
    both = both.reshape(YS, ZS, 2, SHARE, COLS)
    both = jnp.sum(lax.all_to_all(both, "y", 0, 0, tiled=True), axis=0)
    both = jnp.sum(lax.all_to_all(both, "z", 0, 0, tiled=True), axis=0)
    return both[0] / (1.0 + both[1])


def solution(mesh):
    split = Mesh(np.asarray(mesh.devices).reshape(YS, ZS, CS, XS, WS), EV + TILE)
    placed = (
        P(TILE, EV, None),
        P(TILE, EV, None),
        P(TILE, EV, None),
        P(TILE, EV, None, None),
        P(TILE, EV),
        P(),
        P(EV),
        P(EV),
        P(EV, None, TILE),
    )
    return jax.shard_map(on_device, mesh=split, in_specs=placed, out_specs=P(EV, TILE), check_vma=False)
```

time: 95.7 us -> 78.8 us (0.82)
  Pallas kernels: 26.1 us -> 10.4 us
  local copies, waits for them, and re-layouts: 2.49 us -> 1.23 us
    pallas_call x1, Pallas kernels: 24.7 us -> 9.01 us  [maps_of(): pl.pallas_call(work, out_shape=(shares, shares), in_specs=[vmem, vmem, sm...]
    unnamed x9 -> x8, local copies, waits for them, and re-layouts: 2.49 us -> 1.23 us
where the time goes in v2:
time: 78.8 us; the launch traced here: 78.4 us
  blocking collectives  62.1 us (79%)
  Pallas kernels  10.4 us (13%)
  starting transfers between devices  1.92 us (2%)
  waiting for transfers between devices  1.88 us (2%)
  local copies, waits for them, and re-layouts  1.23 us (2%)
    all_to_all x1, blocking collectives, on_device(): arrived = lax.all_to_all(outgoing, TILE, 0, 0, tiled=True)  31.8 us
    all_to_all x1, blocking collectives, on_device(): both = jnp.sum(lax.all_to_all(both, 'z', 0, 0, tiled=True), axis=0)  16.3 us
    all_to_all x1, blocking collectives, on_device(): both = jnp.sum(lax.all_to_all(both, 'y', 0, 0, tiled=True), axis=0)  14 us
    pallas_call x1, Pallas kernels, maps_of(): pl.pallas_call(work, out_shape=(shares, shares), in_specs=[vmem, vmem, sm...  9.01 us
    ppermute x1, starting transfers between devices, on_device(): both = keep + lax.ppermute(send, 'c', [(0, 1), (1, 0)])  1.92 us
    ppermute x1, waiting for transfers between devices, on_device(): both = keep + lax.ppermute(send, 'c', [(0, 1), (1, 0)])  1.88 us
  transfers between devices with their start and end apart: 1, of which 1 were waited for; matrix products, arithmetic and copies ran while one was open for 0% of the time, Pallas kernels for 0%

profile of v2, /device:TPU:2, one launch (start us, length us, event | category | flops | bytes accessed | tf_op | source)
XLA Modules:
  0.0 78.4 jit_solution(15983743430778217176)
XLA Ops:
  0.0 1.4 %pack.1 = f32[8,16,128]{2,1,0:T(8,128)} custom-call(f32[1,2,256]{2,1,0:T(2,128)} %times.1, s32[1,2,256]{2,1,0:T(2,128)} %kernels.1, s32[1,2,256]{2,1,0:T(2,128)} %blocks.1, s32[2,1,256]{2,1,0:T(1,128)} %bitcast.5, s32[1,2]{1,0:T(1,128)} %counts.1), custom_call_target="tpu_custom_call" | custom-call | tf_op jit(solution)/shard_map/pack/pallas_call | solution.py:250
  1.4 0.0 copy-start.1
  1.4 0.0 copy-start.2
  1.4 0.0 copy-start.3
  1.4 31.8 %all_to_all.15.arrived = f32[8,16,128]{2,1,0:T(8,128)S(1)} all-to-all(f32[8,16,128]{2,1,0:T(8,128)} %pack.1), channel_id=1, replica_groups=mesh['y'=4,'z'=8,'c'=2,'x'=4,'w'=2] {'x','w'}, dimensions={0} | all-to-all | bytes 131072 | tf_op jit(solution)/shard_map/all_to_all | solution.py:261
  33.3 0.0 copy-done.1
  33.3 0.0 copy-done.2
  33.3 0.0 copy-done.3
  33.3 0.0 copy-start
  33.3 1.2 %copy-done = f32[2,512,256]{2,1,0:T(8,128)S(1)} copy-done((f32[2,512,256]{2,1,0:T(8,128)S(1)}, f32[2,512,256]{2,1,0:T(8,128)}, u32[]{:S(2)}) %copy-start) | copy-done | bytes 1048600
  34.5 9.0 %maps.1 = (f32[32,2,8,256]{3,2,1,0:T(8,128)S(1)}, f32[32,2,8,256]{3,2,1,0:T(8,128)S(1)}) custom-call(f32[8,16,128]{2,1,0:T(8,128)S(1)} %all_to_all.15.arrived, s32[64,128]{1,0:T(8,128)S(1)} %copy-done.1, f32[2]{0:T(128)S(1)} %copy-done.2, f32[2]{0:T(128)S(1)} %copy-done.3, f32[2,512,256]{2,1,0:T(8,128)S(1)} %copy-done), custom_call_target="tpu_custom_call" | custom-call | tf_op jit(solution)/shard_map/maps/pallas_call | solution.py:230
  43.5 1.9 %collective-permute-start = (f32[32,2,8,256]{3,2,1,0:T(8,128)S(1)}, f32[32,2,8,256]{3,2,1,0:T(8,128)S(1)}, u32[]{:S(2)}, u32[]{:S(2)}) collective-permute-start(f32[32,2,8,256]{3,2,1,0:T(8,128)S(1)} %get-tuple-element.8), channel_id=1, source_target_pairs={{0,8},{8,0},{1,9},{9,1},{2,10},{10,2},{3,11},{11,3},{4,12},{12,4},... | collective-permute-start | bytes 1572872 | tf_op jit(solution)/shard_map/ppermute | solution.py:263
  45.5 1.9 %collective-permute-done = f32[32,2,8,256]{3,2,1,0:T(8,128)S(1)} collective-permute-done((f32[32,2,8,256]{3,2,1,0:T(8,128)S(1)}, f32[32,2,8,256]{3,2,1,0:T(8,128)S(1)}, u32[]{:S(2)}, u32[]{:S(2)}) %collective-permute-start) | collective-permute-done | bytes 524320 | tf_op jit(solution)/shard_map/ppermute | solution.py:263
  47.3 0.1 add.10
  47.4 14.0 %all_to_all.16 = f32[4,8,2,8,256]{4,3,2,1,0:T(8,128)S(1)} all-to-all(f32[4,8,2,8,256]{4,3,2,1,0:T(8,128)S(1)} %bitcast.4), channel_id=1, replica_groups=mesh['y'=4,'z'=8,'c'=2,'x'=4,'w'=2] {'y'}, dimensions={0} | all-to-all | bytes 1048576 | tf_op jit(solution)/shard_map/all_to_all | solution.py:265
  61.5 16.3 %all_to_all.17 = f32[8,2,8,256]{3,2,1,0:T(8,128)S(1)} all-to-all(f32[8,2,8,256]{3,2,1,0:T(8,128)S(1)} %reduce_sum.18), channel_id=1, replica_groups=mesh['y'=4,'z'=8,'c'=2,'x'=4,'w'=2] {'z'}, dimensions={0} | all-to-all | bytes 262144 | tf_op jit(solution)/shard_map/all_to_all | solution.py:266
  77.8 0.6 fusion.1
  (2 shorter events, 0.1 us)
Async XLA Ops:
  1.4 31.8 %copy-start.1 = (s32[64,128]{1,0:T(8,128)S(1)}, s32[64,128]{1,0:T(8,128)}, u32[]{:S(2)}) copy-start(s32[64,128]{1,0:T(8,128)} %table.1) | copy-start | bytes 98308
  1.4 31.8 %copy-start.2 = (f32[2]{0:T(128)S(1)}, f32[2]{0:T(128)}, u32[]{:S(2)}) copy-start(f32[2]{0:T(128)} %source_row.1) | copy-start | bytes 28
  1.4 31.8 %copy-start.3 = (f32[2]{0:T(128)S(1)}, f32[2]{0:T(128)}, u32[]{:S(2)}) copy-start(f32[2]{0:T(128)} %source_col.1) | copy-start | bytes 28
  33.3 1.2 %copy-start = (f32[2,512,256]{2,1,0:T(8,128)S(1)}, f32[2,512,256]{2,1,0:T(8,128)}, u32[]{:S(2)}) copy-start(f32[2,512,256]{2,1,0:T(8,128)} %valid_hbm.1) | copy-start | bytes 3145732
  43.5 3.8 %collective-permute-start = (f32[32,2,8,256]{3,2,1,0:T(8,128)S(1)}, f32[32,2,8,256]{3,2,1,0:T(8,128)S(1)}, u32[]{:S(2)}, u32[]{:S(2)}) collective-permute-start(f32[32,2,8,256]{3,2,1,0:T(8,128)S(1)} %get-tuple-element.8), channel_id=1, source_target_pairs={{0,8},{8,0},{1,9},{9,1},{2,10},{10,2},{3,11},{11,3},{4,12},{12,4},... | collective-permute-start | bytes 1572872 | tf_op jit(solution)/shard_map/ppermute | solution.py:263

commit v3 on v2

v3 whole, which is shorter than its diff:
```python
import functools

import jax
import jax.numpy as jnp
import numpy as np
from jax import lax
from jax.experimental import pallas as pl
from jax.experimental.pallas import tpu as pltpu
from jax.sharding import Mesh
from jax.sharding import PartitionSpec as P

SWEEPS = 4
SMOOTH = 0.024

YS, ZS, CS, XS, WS = 4, 8, 2, 4, 2
EV, TILE = ("y", "z", "c"), "tile"
LISTS = XS * WS
TILE_FIRST, Y_FIRST, Z_FIRST = 5, 2, 4


def order(first, count):
    return [[first ^ i for i in range(count)]]


EVENTS, SLOTS, ROWS, COLS, LANES = 2, 256, 512, 256, 128
KERN = 64
SHARE = ROWS // (YS * ZS * CS)
PAD = 8
EDGE = 8
SPAN = COLS + 2 * EDGE
LINES = ROWS // LANES
BLOCK = 32


def pack(times, kernels, blocks, dests, counts, out):
    lane = lax.broadcasted_iota(jnp.int32, (1, LANES), 1)
    for e in range(EVENTS):
        for h in range(2):
            part = slice(h * LANES, (h + 1) * LANES)
            live = lane + h * LANES < counts[0, e]
            k = 2 * e + h
            out[0, k : k + 1, :] = times[0, e : e + 1, part]
            out[0, 4 + k : 5 + k, :] = jnp.where(live, kernels[0, e : e + 1, part], -1).astype(jnp.float32)
            out[0, 8 + k : 9 + k, :] = blocks[0, e : e + 1, part].astype(jnp.float32)
            out[0, 12 + k : 13 + k, :] = dests[e, :, part].astype(jnp.float32)
    for p in range(1, LISTS):
        out[p] = out[0]


def weight_columns(table):
    columns = jnp.transpose(table[...].astype(jnp.float32)) * (1.0 / 256.0)
    none = jnp.zeros((LANES, KERN), jnp.float32)
    return jnp.concatenate(
        [
            jnp.concatenate([columns[LANES - EDGE :]] + [none[:EDGE]] * 3, axis=1),
            jnp.concatenate([none, columns, none, none], axis=1),
            jnp.concatenate([none, none, columns, none], axis=1),
            jnp.concatenate([none[:EDGE]] * 3 + [columns[:EDGE]], axis=1),
        ],
        axis=0,
    ).astype(jnp.bfloat16)


def build(arrived, by_segment, tile, e, onehot, cells):
    f32, bf16 = jnp.float32, jnp.bfloat16
    pick = lax.broadcasted_iota(jnp.int32, (4 * KERN, SLOTS), 0)
    row_of = lax.broadcasted_iota(jnp.int32, (ROWS, SLOTS), 0)
    for t in range(LISTS):

        def both(k):
            k = k + 2 * e
            return jnp.concatenate([arrived[t, k : k + 1, :], arrived[t, k + 1 : k + 2, :]], axis=1)

        time = both(0)
        kernel = both(4).astype(jnp.int32)
        block = both(8).astype(jnp.int32)
        dest = both(12).astype(jnp.int32)
        seg = dest * 2 + (block & 1) - 2 * tile + 1
        row = block >> 1
        place = (row & (LINES - 1)) * LANES + row // LINES
        choice = jnp.where((kernel >= 0) & (seg >= 0) & (seg < 4), seg * KERN + kernel, -1)
        at = slice(t * SLOTS, (t + 1) * SLOTS)
        onehot[e, :, at] = jnp.where(row_of == place, 1.0, 0.0).astype(bf16)
        picked = jnp.where(pick == choice, 1.0, 0.0).astype(bf16)
        w = jnp.dot(by_segment, picked, preferred_element_type=f32)
        v = w * time
        v_hi = v.astype(bf16)
        cells[e, 0:SPAN, at] = w.astype(bf16)
        cells[e, SPAN : 2 * SPAN, at] = v_hi
        cells[e, 2 * SPAN : 3 * SPAN, at] = (v - v_hi.astype(f32)).astype(bf16)


def total(cells, onehot, e, r):
    sums = lax.dot_general(
        cells[e], onehot[e, r : r + 256], (((1,), (1,)), ((), ())), preferred_element_type=jnp.float32
    )
    return sums[0:SPAN], sums[SPAN : 2 * SPAN] + sums[2 * SPAN : 3 * SPAN]


def start(weight, number, e, r, keeps, adds, change):
    for t in range(r // LANES, r // LANES + 2):
        part = slice(t * LANES - r, (t + 1) * LANES - r)
        first = SMOOTH * number[:, part]
        keeps[e, t] = 1.0 - SMOOTH * weight[:, part]
        adds[e, t] = first
        change[e, t, PAD : PAD + SPAN, :] = first


def beside(tiles, lane):
    first = jnp.where(lane == 0, 0.0, pltpu.roll(tiles[-1], 1, 1))
    last = jnp.where(lane == LANES - 1, 0.0, pltpu.roll(tiles[0], LANES - 1, 1))
    return [first] + tiles[:-1], tiles[1:] + [last]


def laplace_of(buf, e, p, size, lane):
    near = [buf[e, t, PAD + p : PAD + p + size, :] for t in range(LINES)]
    above, below = beside(near, lane)
    out = []
    for t in range(LINES):
        left = buf[e, t, PAD + p - 1 : PAD + p - 1 + size, :]
        right = buf[e, t, PAD + p + 1 : PAD + p + 1 + size, :]
        out.append((left + right) + (above[t] + below[t]) - 4.0 * near[t])
    return out


def work(
    arrived, table, source_row, source_col, valid_hbm, send, keep,
    onehot, cells, keeps, adds, change, curve, valid, stacked, arrivals,
):
    f32 = jnp.float32
    tile = lax.axis_index("tile")
    core = lax.axis_index("c")
    copies = [
        pltpu.make_async_copy(
            valid_hbm.at[e, :, h * LANES : (h + 1) * LANES], valid.at[e, h], arrivals.at[2 * e + h]
        )
        for e in range(EVENTS)
        for h in range(2)
    ]
    for copy in copies:
        copy.start()
    empty = jnp.zeros((PAD, LANES), f32)
    for buf in (change, curve):
        for e in range(EVENTS):
            for t in range(LINES):
                buf[e, t, 0:PAD, :] = empty
                buf[e, t, PAD + SPAN :, :] = empty

    lane = lax.broadcasted_iota(jnp.int32, (1, LANES), 1)
    inside = {
        0: jnp.where(tile == 0, 0.0, 1.0).astype(f32),
        SPAN - EDGE: jnp.where(tile == LISTS - 1, 0.0, 1.0).astype(f32),
    }
    cuts = [0] + list(range(EDGE, SPAN - EDGE, BLOCK)) + [SPAN - EDGE, SPAN]
    parts = [(p, q - p) for p, q in zip(cuts, cuts[1:])]

    def sweep(e):
        for p, size in parts:
            for t, lap in enumerate(laplace_of(change, e, p, size, lane)):
                curve[e, t, PAD + p : PAD + p + size, :] = lap * inside[p] if p in inside else lap
        for p, size in parts:
            for t, bend in enumerate(laplace_of(curve, e, p, size, lane)):
                old = change[e, t, PAD + p : PAD + p + size, :]
                new = keeps[e, t, p : p + size, :] * old + (adds[e, t, p : p + size, :] - SMOOTH * bend)
                change[e, t, PAD + p : PAD + p + size, :] = new * inside[p] if p in inside else new

    lines = lax.broadcasted_iota(jnp.int32, (1, LANES), 1) * LINES
    column = lax.broadcasted_iota(jnp.int32, (LANES, 1), 0) + tile * COLS

    def stack(e):
        for h in range(2):
            p = PAD + EDGE + h * LANES
            near = [change[e, t, p : p + LANES, :] for t in range(LINES)]
            above, below = beside(near, lane)
            off_col = (column + h * LANES).astype(f32) - source_col[e]
            for t in range(LINES):
                left = change[e, t, p - 1 : p - 1 + LANES, :]
                right = change[e, t, p + 1 : p + 1 + LANES, :]
                off_row = (lines + t).astype(f32) - source_row[e]
                inverse = lax.rsqrt(off_row * off_row + off_col * off_col)
                along_row = off_row * inverse + 0.5 * (below[t] - above[t])
                along_col = off_col * inverse + 0.5 * (right - left)
                speed = jnp.sqrt(along_row * along_row + along_col * along_col)
                at = pl.ds(t, LANES, stride=LINES)
                term = valid[e, h, at, :] * jnp.transpose(speed)
                stacked[h, at, :] = term if e == 0 else stacked[h, at, :] + term

    by_segment = weight_columns(table)
    build(arrived, by_segment, tile, 0, onehot, cells)
    start(*total(cells, onehot, 0, 0), 0, 0, keeps, adds, change)
    build(arrived, by_segment, tile, 1, onehot, cells)
    start(*total(cells, onehot, 0, 256), 0, 256, keeps, adds, change)
    sweep(0)
    start(*total(cells, onehot, 1, 0), 1, 0, keeps, adds, change)
    sweep(0)
    start(*total(cells, onehot, 1, 256), 1, 256, keeps, adds, change)
    sweep(0)
    for copy in copies:
        copy.wait()
    stack(0)
    for k in range(SWEEPS - 1):
        sweep(1)
    stack(1)

    def deal(out, core_of):
        def one_share(g, carry):
            at = pl.ds(pl.multiple_of(g * (CS * SHARE) + core_of * SHARE, SHARE), SHARE)
            k = g ^ (Y_FIRST * ZS + Z_FIRST)
            for h in range(2):
                part = slice(h * LANES, (h + 1) * LANES)
                out[k, 0, :, part] = stacked[h, at, :]
                out[k, 1, :, part] = valid[0, h, at, :] + valid[1, h, at, :]
            return carry

        lax.fori_loop(0, YS * ZS, one_share, 0, unroll=8)

    deal(send, 1 - core)
    deal(keep, core)


def maps_of(arrived, table, source_row, source_col, valid):
    f32 = jnp.float32
    shares = jax.ShapeDtypeStruct((YS * ZS, 2, SHARE, COLS), f32)
    vmem, smem = pl.BlockSpec(memory_space=pltpu.VMEM), pl.BlockSpec(memory_space=pltpu.SMEM)
    wide = pltpu.VMEM((EVENTS, LINES, SPAN, LANES), f32)
    padded = pltpu.VMEM((EVENTS, LINES, SPAN + 2 * PAD, LANES), f32)
    return pl.pallas_call(
        work,
        out_shape=(shares, shares),
        in_specs=[vmem, vmem, smem, smem, pl.BlockSpec(memory_space=pltpu.HBM)],
        out_specs=(vmem, vmem),
        scratch_shapes=[
            pltpu.VMEM((EVENTS, ROWS, LISTS * SLOTS), jnp.bfloat16),
            pltpu.VMEM((EVENTS, 3 * SPAN, LISTS * SLOTS), jnp.bfloat16),
            wide, wide, padded, padded,
            pltpu.VMEM((EVENTS, 2, ROWS, LANES), f32),
            pltpu.VMEM((2, ROWS, LANES), f32),
            pltpu.SemaphoreType.DMA((2 * EVENTS,)),
        ],
        compiler_params=pltpu.CompilerParams(vmem_limit_bytes=53760 * 1024),
        name="maps",
    )(arrived, table, source_row, source_col, valid)


def packed(times, kernels, blocks, dests, counts):
    vmem, smem = pl.BlockSpec(memory_space=pltpu.VMEM), pl.BlockSpec(memory_space=pltpu.SMEM)
    return pl.pallas_call(
        pack,
        out_shape=jax.ShapeDtypeStruct((LISTS, 16, LANES), jnp.float32),
        in_specs=[vmem, vmem, vmem, vmem, smem],
        out_specs=vmem,
        name="pack",
    )(times, kernels, blocks, dests, counts)


def on_device(times, kernels, blocks, dests, counts, table, source_row, source_col, valid):
    outgoing = packed(times, kernels, blocks, dests.reshape(EVENTS, 1, SLOTS), counts)
    arrived = lax.all_to_all(outgoing, TILE, 0, 0, tiled=True, axis_index_groups=order(TILE_FIRST, LISTS))
    send, keep = maps_of(arrived, table, source_row, source_col, valid)
    both = keep + lax.ppermute(send, "c", [(0, 1), (1, 0)])
    both = both.reshape(YS, ZS, 2, SHARE, COLS)
    both = jnp.sum(lax.all_to_all(both, "y", 0, 0, tiled=True, axis_index_groups=order(Y_FIRST, YS)), axis=0)
    both = jnp.sum(lax.all_to_all(both, "z", 0, 0, tiled=True, axis_index_groups=order(Z_FIRST, ZS)), axis=0)
    return both[0] / (1.0 + both[1])


def solution(mesh):
    split = Mesh(np.asarray(mesh.devices).reshape(YS, ZS, CS, XS * WS), EV + (TILE,))
    placed = (
        P(TILE, EV, None),
        P(TILE, EV, None),
        P(TILE, EV, None),
        P(TILE, EV, None, None),
        P(TILE, EV),
        P(),
        P(EV),
        P(EV),
        P(EV, None, TILE),
    )
    return jax.shard_map(on_device, mesh=split, in_specs=placed, out_specs=P(EV, TILE), check_vma=False)
```

time: 78.8 us -> 63.7 us (0.81)
  the two profiles are of different devices: /device:TPU:2 before, /device:TPU:4 now
where the time goes in v3:
time: 63.7 us; the launch traced here: 63.3 us
  blocking collectives  49.6 us (78%)
  Pallas kernels  9.15 us (14%)
  starting transfers between devices  1.92 us (3%)
  waiting for transfers between devices  1.88 us (3%)
  other arithmetic  0.74 us (1%)
    all_to_all x1, blocking collectives, on_device(): lax.all_to_all(outgoing, TILE, 0, 0, tiled=True, axis_index_groups=order(...  22.5 us
    all_to_all x1, blocking collectives, on_device(): lax.all_to_all(both, 'z', 0, 0, tiled=True, axis_index_groups=order(Z_FIR...  14.6 us
    all_to_all x1, blocking collectives, on_device(): lax.all_to_all(both, 'y', 0, 0, tiled=True, axis_index_groups=order(Y_FIR...  12.4 us
    pallas_call x1, Pallas kernels, maps_of(): pl.pallas_call(work, out_shape=(shares, shares), in_specs=[vmem, vmem, sm...  7.71 us
    ppermute x1, starting transfers between devices, on_device(): both = keep + lax.ppermute(send, 'c', [(0, 1), (1, 0)])  1.92 us
    ppermute x1, waiting for transfers between devices, on_device(): both = keep + lax.ppermute(send, 'c', [(0, 1), (1, 0)])  1.88 us
    pallas_call x1, Pallas kernels, packed(): pl.pallas_call(pack, out_shape=jax.ShapeDtypeStruct((LISTS, 16, LANES), j...  1.43 us
  transfers between devices with their start and end apart: 1, of which 1 were waited for; matrix products, arithmetic and copies ran while one was open for 0% of the time, Pallas kernels for 0%

profile of v3, /device:TPU:4, one launch (start us, length us, event | category | flops | bytes accessed | tf_op | source)
XLA Modules:
  0.0 63.3 jit_solution(9844675793668373396)
XLA Ops:
  0.0 1.4 %pack.1 = f32[8,16,128]{2,1,0:T(8,128)} custom-call(f32[1,2,256]{2,1,0:T(2,128)} %times.1, s32[1,2,256]{2,1,0:T(2,128)} %kernels.1, s32[1,2,256]{2,1,0:T(2,128)} %blocks.1, s32[2,1,256]{2,1,0:T(1,128)} %bitcast.5, s32[1,2]{1,0:T(1,128)} %counts.1), custom_call_target="tpu_custom_call" | custom-call | tf_op jit(solution)/shard_map/pack/pallas_call | solution.py:247
  1.4 0.0 copy-start
  1.4 0.0 copy-start.1
  1.4 0.0 copy-start.2
  1.4 22.5 %all_to_all.15.arrived = f32[8,16,128]{2,1,0:T(8,128)S(1)} all-to-all(f32[8,16,128]{2,1,0:T(8,128)} %pack.1), channel_id=1, replica_groups={{5,4,7,6,1,0,3,2},{13,12,15,14,9,8,11,10},{21,20,23,22,17,16,19,18},{29..., dimensions={0} | all-to-all | bytes 131072 | tf_op jit(solution)/shard_map/all_to_all | solution.py:258
  24.0 0.0 copy-done
  24.0 0.0 copy-done.1
  24.0 0.0 copy-done.2
  24.0 7.7 %maps.1 = (f32[32,2,8,256]{3,2,1,0:T(8,128)S(1)}, f32[32,2,8,256]{3,2,1,0:T(8,128)S(1)}) custom-call(f32[8,16,128]{2,1,0:T(8,128)S(1)} %all_to_all.15.arrived, s32[64,128]{1,0:T(8,128)S(1)} %copy-done, f32[2]{0:T(128)S(1)} %copy-done.1, f32[2]{0:T(128)S(1)} %copy-done.2, f32[2,512,256]{2,1,0:T(8,128)} %valid_hbm.1), custom_call_target="tpu_custom_call" | custom-call | tf_op jit(solution)/shard_map/maps/pallas_call | solution.py:227
  31.7 1.9 %collective-permute-start = (f32[32,2,8,256]{3,2,1,0:T(8,128)S(1)}, f32[32,2,8,256]{3,2,1,0:T(8,128)S(1)}, u32[]{:S(2)}, u32[]{:S(2)}) collective-permute-start(f32[32,2,8,256]{3,2,1,0:T(8,128)S(1)} %get-tuple-element.8), channel_id=1, source_target_pairs={{0,8},{8,0},{1,9},{9,1},{2,10},{10,2},{3,11},{11,3},{4,12},{12,4},... | collective-permute-start | bytes 1572872 | tf_op jit(solution)/shard_map/ppermute | solution.py:260
  33.6 1.9 %collective-permute-done = f32[32,2,8,256]{3,2,1,0:T(8,128)S(1)} collective-permute-done((f32[32,2,8,256]{3,2,1,0:T(8,128)S(1)}, f32[32,2,8,256]{3,2,1,0:T(8,128)S(1)}, u32[]{:S(2)}, u32[]{:S(2)}) %collective-permute-start) | collective-permute-done | bytes 524320 | tf_op jit(solution)/shard_map/ppermute | solution.py:260
  35.5 0.1 add.10
  35.6 12.4 %all_to_all.16 = f32[4,8,2,8,256]{4,3,2,1,0:T(8,128)S(1)} all-to-all(f32[4,8,2,8,256]{4,3,2,1,0:T(8,128)S(1)} %bitcast.4), channel_id=1, replica_groups={{256,384,0,128},{257,385,1,129},{258,386,2,130},{259,387,3,131},{260,38..., dimensions={0} | all-to-all | bytes 1048576 | tf_op jit(solution)/shard_map/all_to_all | solution.py:262
  48.1 14.6 %all_to_all.17 = f32[8,2,8,256]{3,2,1,0:T(8,128)S(1)} all-to-all(f32[8,2,8,256]{3,2,1,0:T(8,128)S(1)} %reduce_sum.18), channel_id=1, replica_groups={{64,80,96,112,0,16,32,48},{65,81,97,113,1,17,33,49},{66,82,98,114,2,18,..., dimensions={0} | all-to-all | bytes 262144 | tf_op jit(solution)/shard_map/all_to_all | solution.py:263
  62.7 0.6 fusion.1
  (2 shorter events, 0.1 us)
Async XLA Ops:
  1.4 22.5 %copy-start = (s32[64,128]{1,0:T(8,128)S(1)}, s32[64,128]{1,0:T(8,128)}, u32[]{:S(2)}) copy-start(s32[64,128]{1,0:T(8,128)} %table.1) | copy-start | bytes 98308
  1.4 22.5 %copy-start.1 = (f32[2]{0:T(128)S(1)}, f32[2]{0:T(128)}, u32[]{:S(2)}) copy-start(f32[2]{0:T(128)} %source_row.1) | copy-start | bytes 28
  1.4 22.5 %copy-start.2 = (f32[2]{0:T(128)S(1)}, f32[2]{0:T(128)}, u32[]{:S(2)}) copy-start(f32[2]{0:T(128)} %source_col.1) | copy-start | bytes 28
  31.7 3.8 %collective-permute-start = (f32[32,2,8,256]{3,2,1,0:T(8,128)S(1)}, f32[32,2,8,256]{3,2,1,0:T(8,128)S(1)}, u32[]{:S(2)}, u32[]{:S(2)}) collective-permute-start(f32[32,2,8,256]{3,2,1,0:T(8,128)S(1)} %get-tuple-element.8), channel_id=1, source_target_pairs={{0,8},{8,0},{1,9},{9,1},{2,10},{10,2},{3,11},{11,3},{4,12},{12,4},... | collective-permute-start | bytes 1572872 | tf_op jit(solution)/shard_map/ppermute | solution.py:260

commit v4 on v3

--- a/solution.py
+++ b/solution.py
@@ -63,8 +63,8 @@
 
 def build(arrived, by_segment, tile, e, onehot, cells):
     f32, bf16 = jnp.float32, jnp.bfloat16
-    pick = lax.broadcasted_iota(jnp.int32, (4 * KERN, SLOTS), 0)
-    row_of = lax.broadcasted_iota(jnp.int32, (ROWS, SLOTS), 0)
+    pick = lax.broadcasted_iota(jnp.int16, (4 * KERN, SLOTS), 0)
+    row_of = lax.broadcasted_iota(jnp.int16, (ROWS, SLOTS), 0)
     for t in range(LISTS):
 
         def both(k):
@@ -80,8 +80,8 @@
         place = (row & (LINES - 1)) * LANES + row // LINES
         choice = jnp.where((kernel >= 0) & (seg >= 0) & (seg < 4), seg * KERN + kernel, -1)
         at = slice(t * SLOTS, (t + 1) * SLOTS)
-        onehot[e, :, at] = jnp.where(row_of == place, 1.0, 0.0).astype(bf16)
-        picked = jnp.where(pick == choice, 1.0, 0.0).astype(bf16)
+        onehot[e, :, at] = jnp.where(row_of == place.astype(jnp.int16), bf16(1), bf16(0))
+        picked = jnp.where(pick == choice.astype(jnp.int16), bf16(1), bf16(0))
         w = jnp.dot(by_segment, picked, preferred_element_type=f32)
         v = w * time
         v_hi = v.astype(bf16)
@@ -203,16 +203,14 @@
     stack(1)
 
     def deal(out, core_of):
-        def one_share(g, carry):
-            at = pl.ds(pl.multiple_of(g * (CS * SHARE) + core_of * SHARE, SHARE), SHARE)
+        first = pl.multiple_of(core_of * SHARE, SHARE)
+        for g in range(YS * ZS):
+            at = pl.ds(first + g * (CS * SHARE), SHARE)
             k = g ^ (Y_FIRST * ZS + Z_FIRST)
             for h in range(2):
                 part = slice(h * LANES, (h + 1) * LANES)
                 out[k, 0, :, part] = stacked[h, at, :]
                 out[k, 1, :, part] = valid[0, h, at, :] + valid[1, h, at, :]
-            return carry
-
-        lax.fori_loop(0, YS * ZS, one_share, 0, unroll=8)
 
     deal(send, 1 - core)
     deal(keep, core)

time: 63.7 us -> 63.5 us (level)
  no operation moved by 1% of the time
where the time goes in v4:
time: 63.5 us; the launch traced here: 63.1 us
  blocking collectives  49.6 us (78%)
  Pallas kernels  8.94 us (14%)
  starting transfers between devices  1.92 us (3%)
  waiting for transfers between devices  1.88 us (3%)
  other arithmetic  0.74 us (1%)
    all_to_all x1, blocking collectives, on_device(): lax.all_to_all(outgoing, TILE, 0, 0, tiled=True, axis_index_groups=order(...  22.5 us
    all_to_all x1, blocking collectives, on_device(): lax.all_to_all(both, 'z', 0, 0, tiled=True, axis_index_groups=order(Z_FIR...  14.6 us
    all_to_all x1, blocking collectives, on_device(): lax.all_to_all(both, 'y', 0, 0, tiled=True, axis_index_groups=order(Y_FIR...  12.4 us
    pallas_call x1, Pallas kernels, maps_of(): pl.pallas_call(work, out_shape=(shares, shares), in_specs=[vmem, vmem, sm...  7.51 us
    ppermute x1, starting transfers between devices, on_device(): both = keep + lax.ppermute(send, 'c', [(0, 1), (1, 0)])  1.92 us
    ppermute x1, waiting for transfers between devices, on_device(): both = keep + lax.ppermute(send, 'c', [(0, 1), (1, 0)])  1.88 us
    pallas_call x1, Pallas kernels, packed(): pl.pallas_call(pack, out_shape=jax.ShapeDtypeStruct((LISTS, 16, LANES), j...  1.43 us
  transfers between devices with their start and end apart: 1, of which 1 were waited for; matrix products, arithmetic and copies ran while one was open for 0% of the time, Pallas kernels for 0%

profile of v4, /device:TPU:4, one launch (start us, length us, event | category | flops | bytes accessed | tf_op | source)
XLA Modules:
  0.0 63.1 jit_solution(10496592455615966264)
XLA Ops:
  0.0 1.4 %pack.1 = f32[8,16,128]{2,1,0:T(8,128)} custom-call(f32[1,2,256]{2,1,0:T(2,128)} %times.1, s32[1,2,256]{2,1,0:T(2,128)} %kernels.1, s32[1,2,256]{2,1,0:T(2,128)} %blocks.1, s32[2,1,256]{2,1,0:T(1,128)} %bitcast.5, s32[1,2]{1,0:T(1,128)} %counts.1), custom_call_target="tpu_custom_call" | custom-call | tf_op jit(solution)/shard_map/pack/pallas_call | solution.py:245
  1.4 0.0 copy-start
  1.4 0.0 copy-start.1
  1.4 0.0 copy-start.2
  1.4 22.5 %all_to_all.15.arrived = f32[8,16,128]{2,1,0:T(8,128)S(1)} all-to-all(f32[8,16,128]{2,1,0:T(8,128)} %pack.1), channel_id=1, replica_groups={{5,4,7,6,1,0,3,2},{13,12,15,14,9,8,11,10},{21,20,23,22,17,16,19,18},{29..., dimensions={0} | all-to-all | bytes 131072 | tf_op jit(solution)/shard_map/all_to_all | solution.py:256
  24.0 0.0 copy-done
  24.0 0.0 copy-done.1
  24.0 0.0 copy-done.2
  24.0 7.5 %maps.1 = (f32[32,2,8,256]{3,2,1,0:T(8,128)S(1)}, f32[32,2,8,256]{3,2,1,0:T(8,128)S(1)}) custom-call(f32[8,16,128]{2,1,0:T(8,128)S(1)} %all_to_all.15.arrived, s32[64,128]{1,0:T(8,128)S(1)} %copy-done, f32[2]{0:T(128)S(1)} %copy-done.1, f32[2]{0:T(128)S(1)} %copy-done.2, f32[2,512,256]{2,1,0:T(8,128)} %valid_hbm.1), custom_call_target="tpu_custom_call" | custom-call | tf_op jit(solution)/shard_map/maps/pallas_call | solution.py:225
  31.5 1.9 %collective-permute-start = (f32[32,2,8,256]{3,2,1,0:T(8,128)S(1)}, f32[32,2,8,256]{3,2,1,0:T(8,128)S(1)}, u32[]{:S(2)}, u32[]{:S(2)}) collective-permute-start(f32[32,2,8,256]{3,2,1,0:T(8,128)S(1)} %get-tuple-element.8), channel_id=1, source_target_pairs={{0,8},{8,0},{1,9},{9,1},{2,10},{10,2},{3,11},{11,3},{4,12},{12,4},... | collective-permute-start | bytes 1572872 | tf_op jit(solution)/shard_map/ppermute | solution.py:258
  33.4 1.9 %collective-permute-done = f32[32,2,8,256]{3,2,1,0:T(8,128)S(1)} collective-permute-done((f32[32,2,8,256]{3,2,1,0:T(8,128)S(1)}, f32[32,2,8,256]{3,2,1,0:T(8,128)S(1)}, u32[]{:S(2)}, u32[]{:S(2)}) %collective-permute-start) | collective-permute-done | bytes 524320 | tf_op jit(solution)/shard_map/ppermute | solution.py:258
  35.3 0.1 add.10
  35.4 12.4 %all_to_all.16 = f32[4,8,2,8,256]{4,3,2,1,0:T(8,128)S(1)} all-to-all(f32[4,8,2,8,256]{4,3,2,1,0:T(8,128)S(1)} %bitcast.4), channel_id=1, replica_groups={{256,384,0,128},{257,385,1,129},{258,386,2,130},{259,387,3,131},{260,38..., dimensions={0} | all-to-all | bytes 1048576 | tf_op jit(solution)/shard_map/all_to_all | solution.py:260
  47.9 14.6 %all_to_all.17 = f32[8,2,8,256]{3,2,1,0:T(8,128)S(1)} all-to-all(f32[8,2,8,256]{3,2,1,0:T(8,128)S(1)} %reduce_sum.18), channel_id=1, replica_groups={{64,80,96,112,0,16,32,48},{65,81,97,113,1,17,33,49},{66,82,98,114,2,18,..., dimensions={0} | all-to-all | bytes 262144 | tf_op jit(solution)/shard_map/all_to_all | solution.py:261
  62.5 0.6 fusion.1
  (2 shorter events, 0.1 us)
Async XLA Ops:
  1.4 22.5 %copy-start = (s32[64,128]{1,0:T(8,128)S(1)}, s32[64,128]{1,0:T(8,128)}, u32[]{:S(2)}) copy-start(s32[64,128]{1,0:T(8,128)} %table.1) | copy-start | bytes 98308
  1.4 22.5 %copy-start.1 = (f32[2]{0:T(128)S(1)}, f32[2]{0:T(128)}, u32[]{:S(2)}) copy-start(f32[2]{0:T(128)} %source_row.1) | copy-start | bytes 28
  1.4 22.5 %copy-start.2 = (f32[2]{0:T(128)S(1)}, f32[2]{0:T(128)}, u32[]{:S(2)}) copy-start(f32[2]{0:T(128)} %source_col.1) | copy-start | bytes 28
  31.5 3.8 %collective-permute-start = (f32[32,2,8,256]{3,2,1,0:T(8,128)S(1)}, f32[32,2,8,256]{3,2,1,0:T(8,128)S(1)}, u32[]{:S(2)}, u32[]{:S(2)}) collective-permute-start(f32[32,2,8,256]{3,2,1,0:T(8,128)S(1)} %get-tuple-element.8), channel_id=1, source_target_pairs={{0,8},{8,0},{1,9},{9,1},{2,10},{10,2},{3,11},{11,3},{4,12},{12,4},... | collective-permute-start | bytes 1572872 | tf_op jit(solution)/shard_map/ppermute | solution.py:258

commit v5 on v4

--- a/solution.py
+++ b/solution.py
@@ -65,11 +65,13 @@
     f32, bf16 = jnp.float32, jnp.bfloat16
     pick = lax.broadcasted_iota(jnp.int16, (4 * KERN, SLOTS), 0)
     row_of = lax.broadcasted_iota(jnp.int16, (ROWS, SLOTS), 0)
+    rows = [arrived[t] for t in range(LISTS)]
+    choices, times = [], []
     for t in range(LISTS):
 
         def both(k):
             k = k + 2 * e
-            return jnp.concatenate([arrived[t, k : k + 1, :], arrived[t, k + 1 : k + 2, :]], axis=1)
+            return jnp.concatenate([rows[t][k : k + 1, :], rows[t][k + 1 : k + 2, :]], axis=1)
 
         time = both(0)
         kernel = both(4).astype(jnp.int32)
@@ -81,9 +83,13 @@
         choice = jnp.where((kernel >= 0) & (seg >= 0) & (seg < 4), seg * KERN + kernel, -1)
         at = slice(t * SLOTS, (t + 1) * SLOTS)
         onehot[e, :, at] = jnp.where(row_of == place.astype(jnp.int16), bf16(1), bf16(0))
-        picked = jnp.where(pick == choice.astype(jnp.int16), bf16(1), bf16(0))
+        choices.append(choice.astype(jnp.int16))
+        times.append(time)
+    for t in range(0, LISTS, 2):
+        at = slice(t * SLOTS, (t + 2) * SLOTS)
+        picked = jnp.concatenate([jnp.where(pick == c, bf16(1), bf16(0)) for c in choices[t : t + 2]], axis=1)
         w = jnp.dot(by_segment, picked, preferred_element_type=f32)
-        v = w * time
+        v = w * jnp.concatenate(times[t : t + 2], axis=1)
         v_hi = v.astype(bf16)
         cells[e, 0:SPAN, at] = w.astype(bf16)
         cells[e, SPAN : 2 * SPAN, at] = v_hi

time: 63.5 us -> 63.5 us (level)
  no operation moved by 1% of the time
where the time goes in v5:
time: 63.5 us; the launch traced here: 63.1 us
  blocking collectives  49.6 us (78%)
  Pallas kernels  8.95 us (14%)
  starting transfers between devices  1.92 us (3%)
  waiting for transfers between devices  1.88 us (3%)
  other arithmetic  0.74 us (1%)
    all_to_all x1, blocking collectives, on_device(): lax.all_to_all(outgoing, TILE, 0, 0, tiled=True, axis_index_groups=order(...  22.5 us
    all_to_all x1, blocking collectives, on_device(): lax.all_to_all(both, 'z', 0, 0, tiled=True, axis_index_groups=order(Z_FIR...  14.6 us
    all_to_all x1, blocking collectives, on_device(): lax.all_to_all(both, 'y', 0, 0, tiled=True, axis_index_groups=order(Y_FIR...  12.4 us
    pallas_call x1, Pallas kernels, maps_of(): pl.pallas_call(work, out_shape=(shares, shares), in_specs=[vmem, vmem, sm...  7.51 us
    ppermute x1, starting transfers between devices, on_device(): both = keep + lax.ppermute(send, 'c', [(0, 1), (1, 0)])  1.92 us
    ppermute x1, waiting for transfers between devices, on_device(): both = keep + lax.ppermute(send, 'c', [(0, 1), (1, 0)])  1.88 us
    pallas_call x1, Pallas kernels, packed(): pl.pallas_call(pack, out_shape=jax.ShapeDtypeStruct((LISTS, 16, LANES), j...  1.43 us
  transfers between devices with their start and end apart: 1, of which 1 were waited for; matrix products, arithmetic and copies ran while one was open for 0% of the time, Pallas kernels for 0%

profile of v5, /device:TPU:4, one launch (start us, length us, event | category | flops | bytes accessed | tf_op | source)
XLA Modules:
  0.0 63.1 jit_solution(18375960666836343600)
XLA Ops:
  0.0 1.4 %pack.1 = f32[8,16,128]{2,1,0:T(8,128)} custom-call(f32[1,2,256]{2,1,0:T(2,128)} %times.1, s32[1,2,256]{2,1,0:T(2,128)} %kernels.1, s32[1,2,256]{2,1,0:T(2,128)} %blocks.1, s32[2,1,256]{2,1,0:T(1,128)} %bitcast.5, s32[1,2]{1,0:T(1,128)} %counts.1), custom_call_target="tpu_custom_call" | custom-call | tf_op jit(solution)/shard_map/pack/pallas_call | solution.py:251
  1.4 0.0 copy-start
  1.4 0.0 copy-start.1
  1.4 0.0 copy-start.2
  1.4 22.5 %all_to_all.15.arrived = f32[8,16,128]{2,1,0:T(8,128)S(1)} all-to-all(f32[8,16,128]{2,1,0:T(8,128)} %pack.1), channel_id=1, replica_groups={{5,4,7,6,1,0,3,2},{13,12,15,14,9,8,11,10},{21,20,23,22,17,16,19,18},{29..., dimensions={0} | all-to-all | bytes 131072 | tf_op jit(solution)/shard_map/all_to_all | solution.py:262
  24.0 0.0 copy-done
  24.0 0.0 copy-done.1
  24.0 0.0 copy-done.2
  24.0 7.5 %maps.1 = (f32[32,2,8,256]{3,2,1,0:T(8,128)S(1)}, f32[32,2,8,256]{3,2,1,0:T(8,128)S(1)}) custom-call(f32[8,16,128]{2,1,0:T(8,128)S(1)} %all_to_all.15.arrived, s32[64,128]{1,0:T(8,128)S(1)} %copy-done, f32[2]{0:T(128)S(1)} %copy-done.1, f32[2]{0:T(128)S(1)} %copy-done.2, f32[2,512,256]{2,1,0:T(8,128)} %valid_hbm.1), custom_call_target="tpu_custom_call" | custom-call | tf_op jit(solution)/shard_map/maps/pallas_call | solution.py:231
  31.5 1.9 %collective-permute-start = (f32[32,2,8,256]{3,2,1,0:T(8,128)S(1)}, f32[32,2,8,256]{3,2,1,0:T(8,128)S(1)}, u32[]{:S(2)}, u32[]{:S(2)}) collective-permute-start(f32[32,2,8,256]{3,2,1,0:T(8,128)S(1)} %get-tuple-element.8), channel_id=1, source_target_pairs={{0,8},{8,0},{1,9},{9,1},{2,10},{10,2},{3,11},{11,3},{4,12},{12,4},... | collective-permute-start | bytes 1572872 | tf_op jit(solution)/shard_map/ppermute | solution.py:264
  33.4 1.9 %collective-permute-done = f32[32,2,8,256]{3,2,1,0:T(8,128)S(1)} collective-permute-done((f32[32,2,8,256]{3,2,1,0:T(8,128)S(1)}, f32[32,2,8,256]{3,2,1,0:T(8,128)S(1)}, u32[]{:S(2)}, u32[]{:S(2)}) %collective-permute-start) | collective-permute-done | bytes 524320 | tf_op jit(solution)/shard_map/ppermute | solution.py:264
  35.3 0.1 add.10
  35.4 12.4 %all_to_all.16 = f32[4,8,2,8,256]{4,3,2,1,0:T(8,128)S(1)} all-to-all(f32[4,8,2,8,256]{4,3,2,1,0:T(8,128)S(1)} %bitcast.4), channel_id=1, replica_groups={{256,384,0,128},{257,385,1,129},{258,386,2,130},{259,387,3,131},{260,38..., dimensions={0} | all-to-all | bytes 1048576 | tf_op jit(solution)/shard_map/all_to_all | solution.py:266
  47.9 14.6 %all_to_all.17 = f32[8,2,8,256]{3,2,1,0:T(8,128)S(1)} all-to-all(f32[8,2,8,256]{3,2,1,0:T(8,128)S(1)} %reduce_sum.18), channel_id=1, replica_groups={{64,80,96,112,0,16,32,48},{65,81,97,113,1,17,33,49},{66,82,98,114,2,18,..., dimensions={0} | all-to-all | bytes 262144 | tf_op jit(solution)/shard_map/all_to_all | solution.py:267
  62.5 0.6 fusion.1
  (2 shorter events, 0.1 us)
Async XLA Ops:
  1.4 22.5 %copy-start = (s32[64,128]{1,0:T(8,128)S(1)}, s32[64,128]{1,0:T(8,128)}, u32[]{:S(2)}) copy-start(s32[64,128]{1,0:T(8,128)} %table.1) | copy-start | bytes 98308
  1.4 22.5 %copy-start.1 = (f32[2]{0:T(128)S(1)}, f32[2]{0:T(128)}, u32[]{:S(2)}) copy-start(f32[2]{0:T(128)} %source_row.1) | copy-start | bytes 28
  1.4 22.5 %copy-start.2 = (f32[2]{0:T(128)S(1)}, f32[2]{0:T(128)}, u32[]{:S(2)}) copy-start(f32[2]{0:T(128)} %source_col.1) | copy-start | bytes 28
  31.5 3.8 %collective-permute-start = (f32[32,2,8,256]{3,2,1,0:T(8,128)S(1)}, f32[32,2,8,256]{3,2,1,0:T(8,128)S(1)}, u32[]{:S(2)}, u32[]{:S(2)}) collective-permute-start(f32[32,2,8,256]{3,2,1,0:T(8,128)S(1)} %get-tuple-element.8), channel_id=1, source_target_pairs={{0,8},{8,0},{1,9},{9,1},{2,10},{10,2},{3,11},{11,3},{4,12},{12,4},... | collective-permute-start | bytes 1572872 | tf_op jit(solution)/shard_map/ppermute | solution.py:264

commit v6 on v5

--- a/solution.py
+++ b/solution.py
@@ -29,7 +29,7 @@
 EDGE = 8
 SPAN = COLS + 2 * EDGE
 LINES = ROWS // LANES
-BLOCK = 32
+BLOCK = 128
 
 
 def pack(times, kernels, blocks, dests, counts, out):
@@ -85,11 +85,11 @@
         onehot[e, :, at] = jnp.where(row_of == place.astype(jnp.int16), bf16(1), bf16(0))
         choices.append(choice.astype(jnp.int16))
         times.append(time)
-    for t in range(0, LISTS, 2):
-        at = slice(t * SLOTS, (t + 2) * SLOTS)
-        picked = jnp.concatenate([jnp.where(pick == c, bf16(1), bf16(0)) for c in choices[t : t + 2]], axis=1)
+    for t in range(0, LISTS, 4):
+        at = slice(t * SLOTS, (t + 4) * SLOTS)
+        picked = jnp.concatenate([jnp.where(pick == c, bf16(1), bf16(0)) for c in choices[t : t + 4]], axis=1)
         w = jnp.dot(by_segment, picked, preferred_element_type=f32)
-        v = w * jnp.concatenate(times[t : t + 2], axis=1)
+        v = w * jnp.concatenate(times[t : t + 4], axis=1)
         v_hi = v.astype(bf16)
         cells[e, 0:SPAN, at] = w.astype(bf16)
         cells[e, SPAN : 2 * SPAN, at] = v_hi

time: 63.5 us -> 63.5 us (level)
  no operation moved by 1% of the time
where the time goes in v6:
time: 63.5 us; the launch traced here: 63.1 us
  blocking collectives  49.6 us (78%)
  Pallas kernels  8.97 us (14%)
  starting transfers between devices  1.92 us (3%)
  waiting for transfers between devices  1.88 us (3%)
  other arithmetic  0.74 us (1%)
    all_to_all x1, blocking collectives, on_device(): lax.all_to_all(outgoing, TILE, 0, 0, tiled=True, axis_index_groups=order(...  22.5 us
    all_to_all x1, blocking collectives, on_device(): lax.all_to_all(both, 'z', 0, 0, tiled=True, axis_index_groups=order(Z_FIR...  14.6 us
    all_to_all x1, blocking collectives, on_device(): lax.all_to_all(both, 'y', 0, 0, tiled=True, axis_index_groups=order(Y_FIR...  12.4 us
    pallas_call x1, Pallas kernels, maps_of(): pl.pallas_call(work, out_shape=(shares, shares), in_specs=[vmem, vmem, sm...  7.54 us
    ppermute x1, starting transfers between devices, on_device(): both = keep + lax.ppermute(send, 'c', [(0, 1), (1, 0)])  1.92 us
    ppermute x1, waiting for transfers between devices, on_device(): both = keep + lax.ppermute(send, 'c', [(0, 1), (1, 0)])  1.88 us
    pallas_call x1, Pallas kernels, packed(): pl.pallas_call(pack, out_shape=jax.ShapeDtypeStruct((LISTS, 16, LANES), j...  1.43 us
  transfers between devices with their start and end apart: 1, of which 1 were waited for; matrix products, arithmetic and copies ran while one was open for 0% of the time, Pallas kernels for 0%

profile of v6, /device:TPU:4, one launch (start us, length us, event | category | flops | bytes accessed | tf_op | source)
XLA Modules:
  0.0 63.1 jit_solution(11712385046947937543)
XLA Ops:
  0.0 1.4 %pack.1 = f32[8,16,128]{2,1,0:T(8,128)} custom-call(f32[1,2,256]{2,1,0:T(2,128)} %times.1, s32[1,2,256]{2,1,0:T(2,128)} %kernels.1, s32[1,2,256]{2,1,0:T(2,128)} %blocks.1, s32[2,1,256]{2,1,0:T(1,128)} %bitcast.5, s32[1,2]{1,0:T(1,128)} %counts.1), custom_call_target="tpu_custom_call" | custom-call | tf_op jit(solution)/shard_map/pack/pallas_call | solution.py:251
  1.4 0.0 copy-start
  1.4 0.0 copy-start.1
  1.4 0.0 copy-start.2
  1.4 22.5 %all_to_all.15.arrived = f32[8,16,128]{2,1,0:T(8,128)S(1)} all-to-all(f32[8,16,128]{2,1,0:T(8,128)} %pack.1), channel_id=1, replica_groups={{5,4,7,6,1,0,3,2},{13,12,15,14,9,8,11,10},{21,20,23,22,17,16,19,18},{29..., dimensions={0} | all-to-all | bytes 131072 | tf_op jit(solution)/shard_map/all_to_all | solution.py:262
  24.0 0.0 copy-done
  24.0 0.0 copy-done.1
  24.0 0.0 copy-done.2
  24.0 7.5 %maps.1 = (f32[32,2,8,256]{3,2,1,0:T(8,128)S(1)}, f32[32,2,8,256]{3,2,1,0:T(8,128)S(1)}) custom-call(f32[8,16,128]{2,1,0:T(8,128)S(1)} %all_to_all.15.arrived, s32[64,128]{1,0:T(8,128)S(1)} %copy-done, f32[2]{0:T(128)S(1)} %copy-done.1, f32[2]{0:T(128)S(1)} %copy-done.2, f32[2,512,256]{2,1,0:T(8,128)} %valid_hbm.1), custom_call_target="tpu_custom_call" | custom-call | tf_op jit(solution)/shard_map/maps/pallas_call | solution.py:231
  31.5 1.9 %collective-permute-start = (f32[32,2,8,256]{3,2,1,0:T(8,128)S(1)}, f32[32,2,8,256]{3,2,1,0:T(8,128)S(1)}, u32[]{:S(2)}, u32[]{:S(2)}) collective-permute-start(f32[32,2,8,256]{3,2,1,0:T(8,128)S(1)} %get-tuple-element.8), channel_id=1, source_target_pairs={{0,8},{8,0},{1,9},{9,1},{2,10},{10,2},{3,11},{11,3},{4,12},{12,4},... | collective-permute-start | bytes 1572872 | tf_op jit(solution)/shard_map/ppermute | solution.py:264
  33.5 1.9 %collective-permute-done = f32[32,2,8,256]{3,2,1,0:T(8,128)S(1)} collective-permute-done((f32[32,2,8,256]{3,2,1,0:T(8,128)S(1)}, f32[32,2,8,256]{3,2,1,0:T(8,128)S(1)}, u32[]{:S(2)}, u32[]{:S(2)}) %collective-permute-start) | collective-permute-done | bytes 524320 | tf_op jit(solution)/shard_map/ppermute | solution.py:264
  35.3 0.1 add.10
  35.4 12.4 %all_to_all.16 = f32[4,8,2,8,256]{4,3,2,1,0:T(8,128)S(1)} all-to-all(f32[4,8,2,8,256]{4,3,2,1,0:T(8,128)S(1)} %bitcast.4), channel_id=1, replica_groups={{256,384,0,128},{257,385,1,129},{258,386,2,130},{259,387,3,131},{260,38..., dimensions={0} | all-to-all | bytes 1048576 | tf_op jit(solution)/shard_map/all_to_all | solution.py:266
  47.9 14.6 %all_to_all.17 = f32[8,2,8,256]{3,2,1,0:T(8,128)S(1)} all-to-all(f32[8,2,8,256]{3,2,1,0:T(8,128)S(1)} %reduce_sum.18), channel_id=1, replica_groups={{64,80,96,112,0,16,32,48},{65,81,97,113,1,17,33,49},{66,82,98,114,2,18,..., dimensions={0} | all-to-all | bytes 262144 | tf_op jit(solution)/shard_map/all_to_all | solution.py:267
  62.5 0.6 fusion.1
  (2 shorter events, 0.0 us)
Async XLA Ops:
  1.4 22.5 %copy-start = (s32[64,128]{1,0:T(8,128)S(1)}, s32[64,128]{1,0:T(8,128)}, u32[]{:S(2)}) copy-start(s32[64,128]{1,0:T(8,128)} %table.1) | copy-start | bytes 98308
  1.4 22.5 %copy-start.1 = (f32[2]{0:T(128)S(1)}, f32[2]{0:T(128)}, u32[]{:S(2)}) copy-start(f32[2]{0:T(128)} %source_row.1) | copy-start | bytes 28
  1.4 22.5 %copy-start.2 = (f32[2]{0:T(128)S(1)}, f32[2]{0:T(128)}, u32[]{:S(2)}) copy-start(f32[2]{0:T(128)} %source_col.1) | copy-start | bytes 28
  31.5 3.8 %collective-permute-start = (f32[32,2,8,256]{3,2,1,0:T(8,128)S(1)}, f32[32,2,8,256]{3,2,1,0:T(8,128)S(1)}, u32[]{:S(2)}, u32[]{:S(2)}) collective-permute-start(f32[32,2,8,256]{3,2,1,0:T(8,128)S(1)} %get-tuple-element.8), channel_id=1, source_target_pairs={{0,8},{8,0},{1,9},{9,1},{2,10},{10,2},{3,11},{11,3},{4,12},{12,4},... | collective-permute-start | bytes 1572872 | tf_op jit(solution)/shard_map/ppermute | solution.py:264
